TPU v7x, 128 devices: a whole 4x4x4 slice. The times are simulated.
128 devices in a mesh: grp: 8 (over z, core), sub: 16 (over y, x).
Axes of the slice: x: 4, y: 4, z: 4, core: 2. Of those that a mesh axis runs over, the one named last changes fastest.
Arguments:
- potential: float32 [2048, 4096], P(('grp', 'sub')), may hold values from -6 to 6
- right_side: float32 [2048, 4096], P(('grp', 'sub')), may hold values from -6.5 to 6.5
- permeability: float32 [2048, 4096], P(('grp', 'sub')), may hold values from 1 to 10
- new_owner: int32 [2048], replicated, may hold values from 0 to 127, as said below
- neighbours: int32 [6, 2048], replicated, may hold values from -1 to 2047, as said below
Outputs:
- new_potential: float32 [3072, 4096], P(('grp', 'sub'))
Inputs may be any that keep to these rules, and one draw needn't show every extreme that they name: `new_owner`: owners never fall as the block id rises. Device d's blocks begin at d * 16 + s with s from -4 to 4 (0 for device 0), so each device gets 16 - 2 * 4 to 24 blocks, and some device gets exactly 24. If n = neighbours[f, b] is not -1 then neighbours[f xor 1, n] = b and n lies within 4 of b; the faces 0 and 1 link blocks exactly 4 apart.
All inputs are finite; a program needn't handle non-finite values.
Results may differ from a plain program's by a relative error of at most 0.00024.
Values sent between devices are 32-bit elements; how exact they have to be, the bound alone decides.
A program may use at most 128 MiB of HBM per device.

v0:
```python
import jax
import jax.numpy as jnp
from jax import lax
from jax.sharding import PartitionSpec as P

BE = 16
LAYER = 4
NPRE = 2
NPOST = 2
CSWEEP = 4


RELAX_FINE = 0.8
RELAX_COARSE = 0.7
OPPOSITE = (1, 0, 3, 2, 5, 4)


def passed_along(shard, axis, by):
    length = lax.axis_size(axis)
    pairs = [(i, i + by) for i in range(length) if 0 <= i + by < length]
    return lax.ppermute(shard, axis, pairs)


def face_one(values, face_index):
    slots_here, block_edge, plane_cells = values.shape
    if face_index == 0:
        return values[:, 0, :]
    if face_index == 1:
        return values[:, block_edge - 1, :]
    if face_index == 2:
        return values[:, :, :block_edge].reshape(slots_here, plane_cells)
    if face_index == 3:
        return values[:, :, plane_cells - block_edge :].reshape(slots_here, plane_cells)
    if face_index == 4:
        return values[:, :, 0::block_edge].reshape(slots_here, plane_cells)
    return values[:, :, block_edge - 1 :: block_edge].reshape(slots_here, plane_cells)


def face_tiles(values):
    return jnp.stack([face_one(values, face_index) for face_index in range(6)], axis=1)


def beside(values, ghosts):
    slots_here, block_edge, plane_cells = values.shape
    zero_column = jnp.zeros((slots_here, block_edge, 1), values.dtype)
    column_pos = lax.broadcasted_iota(jnp.int32, (1, 1, plane_cells), 2) % block_edge
    lower_z = jnp.concatenate([ghosts[:, 0][:, None, :], values[:, :-1, :]], axis=1)
    upper_z = jnp.concatenate([values[:, 1:, :], ghosts[:, 1][:, None, :]], axis=1)
    lower_y = jnp.concatenate(
        [ghosts[:, 2].reshape(slots_here, block_edge, block_edge), values[:, :, :-block_edge]],
        axis=2,
    )
    upper_y = jnp.concatenate(
        [values[:, :, block_edge:], ghosts[:, 3].reshape(slots_here, block_edge, block_edge)],
        axis=2,
    )
    ghost_lower_x = jnp.repeat(
        ghosts[:, 4].reshape(slots_here, block_edge, block_edge), block_edge, axis=2
    )
    ghost_upper_x = jnp.repeat(
        ghosts[:, 5].reshape(slots_here, block_edge, block_edge), block_edge, axis=2
    )
    lower_x = jnp.where(
        column_pos == 0, ghost_lower_x, jnp.concatenate([zero_column, values[:, :, :-1]], axis=2)
    )
    upper_x = jnp.where(
        column_pos == block_edge - 1,
        ghost_upper_x,
        jnp.concatenate([values[:, :, 1:], zero_column], axis=2),
    )
    return [lower_z, upper_z, lower_y, upper_y, lower_x, upper_x]


def couplings(perm_field, perm_ghosts):
    return [
        2.0 * perm_field * nearby / (perm_field + nearby)
        for nearby in beside(perm_field, perm_ghosts)
    ]


def apply_operator(values, ghosts, coupling, diagonal):
    result = diagonal * values
    for factor, nearby in zip(coupling, beside(values, ghosts)):
        result = result - factor * nearby
    return result


def local(potential, right_side, permeability, new_owner, neighbours):
    own_blocks, cells_total = potential.shape
    block_edge = BE
    plane_cells = block_edge * block_edge
    shift_len = own_blocks // 4
    slots_n = own_blocks + 2 * shift_len
    blocks_total = new_owner.shape[0]
    sub_count = lax.axis_size("sub")
    device_count = lax.axis_size("grp") * sub_count
    group_index = lax.axis_index("grp")
    my_index = group_index * sub_count + lax.axis_index("sub")
    bounds = jnp.sum(
        (new_owner[None, :] < jnp.arange(device_count + 1, dtype=jnp.int32)[:, None]).astype(
            jnp.int32
        ),
        axis=1,
    )
    my_start = bounds[my_index]
    my_end = bounds[my_index + 1]
    my_count = my_end - my_start
    out_pos = jnp.arange(slots_n, dtype=jnp.int32)
    live_slot = out_pos < my_count
    offset = my_start - my_index * own_blocks + shift_len
    stacked = jnp.stack([potential, right_side, permeability]).reshape(
        3, own_blocks, block_edge, plane_cells
    )
    arrivals = []
    for step_by in (1, -1):
        piece = stacked[:, own_blocks - shift_len :] if step_by == 1 else stacked[:, :shift_len]
        arrivals.append(passed_along(piece, ("grp", "sub"), step_by))
    window = jnp.concatenate(
        [
            arrivals[0],
            stacked,
            arrivals[1],
            jnp.zeros((3, slots_n, block_edge, plane_cells), jnp.float32),
        ],
        axis=1,
    )
    moved = lax.dynamic_slice_in_dim(window, offset, slots_n, axis=1)
    live_mask = live_slot[:, None, None]
    values = jnp.where(live_mask, moved[0], 0.0)
    source = jnp.where(live_mask, moved[1], 0.0)
    perm_field = jnp.where(live_mask, moved[2], 1.0)
    solve_cells = live_slot[:, None, None]
    slot_pos = jnp.arange(slots_n, dtype=jnp.int32)
    padded_table = jnp.concatenate([neighbours, jnp.full((6, slots_n), -1, jnp.int32)], axis=1)
    slot_table = lax.dynamic_slice(padded_table, (0, my_start), (6, slots_n))
    slot_table = jnp.where(live_slot[None, :], slot_table, -1)
    relative = jnp.where(slot_table >= 0, slot_table - (my_start + slot_pos)[None, :], 99)
    near_offsets = [k for k in range(-LAYER, LAYER + 1) if k != 0]
    face_offsets = [[-LAYER, LAYER], [-LAYER, LAYER]] + [near_offsets] * 4

    def gather_ghosts(face_set):
        arrived = []
        for step_by in (1, -1):
            arrived.append(passed_along(face_set, ("grp", "sub"), step_by))
        prev_count = my_start - bounds[jnp.maximum(my_index - 1, 0)]
        lower_rim = lax.dynamic_slice_in_dim(
            arrived[0], jnp.maximum(prev_count - LAYER, 0), LAYER, 0
        )
        upper_rim = arrived[1][:LAYER]
        padding = jnp.zeros((LAYER, 6, plane_cells), jnp.float32)
        extended = jnp.concatenate([lower_rim, face_set, padding], axis=0)
        extended = lax.dynamic_update_slice_in_dim(extended, upper_rim, LAYER + my_count, 0)
        tiles = []
        for face_index in range(6):
            source_face = OPPOSITE[face_index]
            gathered = jnp.zeros((slots_n, plane_cells), jnp.float32)
            for step_k in face_offsets[face_index]:
                candidate = extended[LAYER + step_k : LAYER + step_k + slots_n, source_face]
                gathered = jnp.where((relative[face_index] == step_k)[:, None], candidate, gathered)
            tiles.append(gathered)
        return jnp.stack(tiles, axis=1)

    boundary = (slot_table < 0).T[:, :, None]
    perm_faces = face_tiles(perm_field)
    perm_ghosts = jnp.where(boundary, perm_faces, gather_ghosts(perm_faces))
    coupling = couplings(perm_field, perm_ghosts)
    diagonal = coupling[0]
    for factor in coupling[1:]:
        diagonal = diagonal + factor

    def smooth(current):
        ghosts = gather_ghosts(face_tiles(current))
        return (
            current
            + RELAX_FINE * (source - apply_operator(current, ghosts, coupling, diagonal)) / diagonal
        )

    for sweep in range(NPRE):
        values = smooth(values)
    residual = source - apply_operator(
        values, gather_ghosts(face_tiles(values)), coupling, diagonal
    )
    coarse_rhs = jnp.where(live_slot, jnp.sum(residual, axis=(1, 2)), 0.0)
    links = jnp.stack(
        [jnp.sum(face_one(coupling[face_index], face_index), axis=1) for face_index in range(6)]
    )
    links = jnp.where(live_slot[None, :], links, 0.0)
    got_rhs, got_links = (
        lax.all_gather(coarse_rhs, "sub", axis=0, tiled=True),
        lax.all_gather(links, "sub", axis=1, tiled=True),
    )
    total_rhs, total_links = lax.psum((jnp.sum(got_rhs), jnp.sum(got_links)), "grp")
    source_devices = group_index * sub_count + jnp.arange(sub_count, dtype=jnp.int32)
    lower_bound = bounds[group_index * sub_count]
    upper_bound = bounds[(group_index + 1) * sub_count]
    level_shift = total_rhs / total_links
    slot_ids = jnp.take(bounds, source_devices)[:, None] + slot_pos[None, :]
    slot_ok = slot_ids < jnp.take(bounds, source_devices + 1)[:, None]
    targets = jnp.where(slot_ok, slot_ids, blocks_total).reshape(-1)
    full_rhs = jnp.zeros((blocks_total + 1,), jnp.float32).at[targets].set(got_rhs)[:blocks_total]
    full_links = (
        jnp.zeros((6, blocks_total + 1), jnp.float32)
        .at[:, targets]
        .set(got_links)[:, :blocks_total]
    )
    block_ids = jnp.arange(blocks_total, dtype=jnp.int32)
    inside = (block_ids >= lower_bound) & (block_ids < upper_bound)
    full_diag = jnp.where(inside, jnp.sum(full_links, axis=0), 1.0)
    padded_len = blocks_total + 2 * LAYER + 1
    positions = jnp.where(neighbours >= 0, neighbours + LAYER, padded_len - 1)
    current = jnp.zeros((padded_len,), jnp.float32)
    for sweep in range(CSWEEP):
        if sweep > 0:
            refresh_current = current
            for refresh_step_by in (1, -1):
                send_at = upper_bound if refresh_step_by == 1 else lower_bound + LAYER
                recv_at = lower_bound if refresh_step_by == 1 else upper_bound + LAYER
                refresh_piece = lax.dynamic_slice_in_dim(refresh_current, send_at, LAYER, 0)
                landed = passed_along(refresh_piece, "grp", refresh_step_by)
                refresh_current = lax.dynamic_update_slice_in_dim(
                    refresh_current, landed, recv_at, 0
                )
            current = refresh_current
        inner = current[LAYER : LAYER + blocks_total]
        product = full_diag * inner - jnp.sum(full_links * current[positions], axis=0)
        inner = jnp.where(inside, inner + RELAX_COARSE * (full_rhs - product) / full_diag, 0.0)
        current = jnp.concatenate(
            [jnp.zeros((LAYER,), jnp.float32), inner, jnp.zeros((LAYER + 1,), jnp.float32)]
        )
    spread = jnp.concatenate([current, jnp.zeros((slots_n,), jnp.float32)])
    correction = jnp.where(
        live_slot, lax.dynamic_slice_in_dim(spread, my_start + LAYER, slots_n, 0) + level_shift, 0.0
    )
    values = values + correction[:, None, None]
    for sweep in range(NPOST):
        values = smooth(values)
    return jnp.where(solve_cells, values, 0.0).reshape(slots_n, cells_total)


def solution(mesh):
    in_specs = (P(("grp", "sub"), None), P(("grp", "sub"), None), P(("grp", "sub"), None), P(), P())
    out_specs = P(("grp", "sub"), None)
    return jax.shard_map(local, mesh=mesh, in_specs=in_specs, out_specs=out_specs, check_vma=False)
```

profile of v0, /device:TPU:1, one launch (start us, length us, event | category | flops | bytes accessed | tf_op | source)
XLA Modules:
  0.0 838.4 jit_solution(804349840754270055)
XLA Ops:
  1.4 3.9 collective-permute-start
  5.4 6.2 collective-permute-start.1
  28.3 68.0 %gather_fusion = f32[12288]{0:T(1024)S(1)} fusion(f32[2057]{0:T(1024)S(1)} %broadcast_in_dim.1311, s32[12288]{0:T(1024)S(1)} %broadcast_clamp_fusion), kind=kCustom, calls=%fused_computation.2 | custom fusion | bytes 147456 | tf_op jit(solution)/shard_map/gather | solution.py:225
  118.0 7.0 collective-permute-start.5
  127.8 7.4 collective-permute-start.3
  147.0 3.5 reshape.1684
  152.7 3.5 reshape.1685
  162.3 3.5 reshape.1686
  170.2 3.7 reshape.1687
  185.6 4.6 fusion.17
  200.8 7.0 collective-permute-start.7
  215.2 16.9 %all-gather = f32[16,24,6]{1,2,0:T(8,128)S(1)} all-gather(f32[1,24,6]{1,2,0:T(8,128)S(1)} %select_bitcast_fusion.1), channel_id=1, replica_groups=mesh['grp'=8,'sub'=16] {'sub'}, dimensions={0}, use_global_device_ids=true | all-gather | bytes 9792 | tf_op jit(solution)/shard_map/all_gather | solution.py:190
  255.3 3.5 reshape.1688
  273.0 3.5 reshape.1689
  317.0 3.3 collective-permute-start.8
  320.3 5.9 collective-permute-start.9
  371.0 3.5 reshape.1690
  390.2 3.5 reshape.1691
  400.5 42.2 %all-reduce.13 = f32[384]{0:T(512)S(1)} all-reduce(f32[384]{0:T(512)S(1)} %select_dynamic-update-slice_fusion), channel_id=1, replica_groups=mesh['grp'=8,'sub'=16] {'sub'}, use_global_device_ids=true, to_apply=%add.13 | all-reduce | flops 384 | bytes 3072
  443.4 3.1 scatter_custom_fusion
  447.9 6.4 collective-permute-start.10
  454.4 12.0 %all-reduce.14 = (f32[]{:T(128)}, f32[]{:T(128)}) all-reduce(f32[]{:T(128)} %reduce_sum.148, f32[]{:T(128)} %reduce_sum.149), channel_id=1, replica_groups=mesh['grp'=8,'sub'=16] {'grp'}, use_global_device_ids=true, to_apply=%region_16.18 | all-reduce | flops 2 | bytes 16 | tf_op jit(solution)/shard_map/psum | solution.py:192
  468.1 3.6 collective-permute-start.11
  473.3 68.0 %gather_fusion.1 = f32[12288]{0:T(1024)S(1)} fusion(f32[2057]{0:T(1024)S(1)} %dynamic_update_slice.41, s32[12288]{0:T(1024)S(1)} %broadcast_clamp_fusion), kind=kCustom, calls=%fused_computation.3 | custom fusion | bytes 147456 | tf_op jit(solution)/shard_map/gather | solution.py:225
  551.2 2.9 collective-permute-done.13
  554.3 68.0 %gather_fusion.2 = f32[12288]{0:T(1024)S(1)} fusion(f32[2057]{0:T(1024)S(1)} %dynamic_update_slice.43, s32[12288]{0:T(1024)S(1)} %broadcast_clamp_fusion), kind=kCustom, calls=%fused_computation.4 | custom fusion | bytes 147456 | tf_op jit(solution)/shard_map/gather | solution.py:225
  635.3 68.0 %gather_fusion.3 = f32[12288]{0:T(1024)S(1)} fusion(f32[2057]{0:T(1024)S(1)} %dynamic_update_slice.45, s32[12288]{0:T(1024)S(1)} %broadcast_clamp_fusion), kind=kCustom, calls=%fused_computation.5 | custom fusion | bytes 147456 | tf_op jit(solution)/shard_map/gather | solution.py:225
  713.7 7.0 collective-permute-start.17
  733.0 3.5 reshape.1692
  743.5 3.5 reshape.1693
  774.0 7.0 collective-permute-start.19
  827.6 3.5 reshape.1695
  (927 shorter events, 361.9 us)
Async XLA Ops:
  1.4 101.4 %collective-permute-start = (f32[3,4,16,256]{3,2,1,0:T(8,128)S(1)}, f32[3,4,16,256]{3,2,1,0:T(8,128)S(1)}, u32[]{:S(2)}, u32[]{:S(2)}) collective-permute-start(f32[3,4,16,256]{3,2,1,0:T(8,128)S(1)} %get-tuple-element.20), channel_id=1, source_target_pairs={{0,1},{1,2},{2,3},{3,4},{4,5},{5,6},{6,7},{7,8},{8,9},{9,10},{10,1... | collective-permute-start | bytes 589832 | tf_op jit(solution)/shard_map/ppermute | solution.py:21
  5.4 97.6 %collective-permute-start.1 = (f32[3,4,16,256]{3,2,1,0:T(8,128)S(1)}, f32[3,4,16,256]{3,2,1,0:T(8,128)S(1)}, u32[]{:S(2)}, u32[]{:S(2)}) collective-permute-start(f32[3,4,16,256]{3,2,1,0:T(8,128)S(1)} %get-tuple-element.19), channel_id=1, source_target_pairs={{1,0},{2,1},{3,2},{4,3},{5,4},{6,5},{7,6},{8,7},{9,8},{10,9},{11,1... | collective-permute-start | bytes 589832 | tf_op jit(solution)/shard_map/ppermute | solution.py:21
  17.4 165.4 %copy-start.101 = (pred[24]{0:T(512)(128)(4,1)}, pred[24]{0:T(512)(128)(4,1)S(1)}, u32[]{:S(2)}) copy-start(pred[24]{0:T(512)(128)(4,1)S(1)} %get-tuple-element.274) | copy-start | bytes 76
  17.4 166.0 %copy-start.121 = (pred[24]{0:T(512)(128)(4,1)}, pred[24]{0:T(512)(128)(4,1)S(1)}, u32[]{:S(2)}) copy-start(pred[24]{0:T(512)(128)(4,1)S(1)} %get-tuple-element.275) | copy-start | bytes 76
  18.1 164.8 %copy-start.103 = (pred[24]{0:T(512)(128)(4,1)}, pred[24]{0:T(512)(128)(4,1)S(1)}, u32[]{:S(2)}) copy-start(pred[24]{0:T(512)(128)(4,1)S(1)} %get-tuple-element.250) | copy-start | bytes 76
  18.1 164.8 %copy-start.105 = (pred[24]{0:T(512)(128)(4,1)}, pred[24]{0:T(512)(128)(4,1)S(1)}, u32[]{:S(2)}) copy-start(pred[24]{0:T(512)(128)(4,1)S(1)} %get-tuple-element.251) | copy-start | bytes 76
  18.1 164.8 %copy-start.108 = (pred[24]{0:T(512)(128)(4,1)}, pred[24]{0:T(512)(128)(4,1)S(1)}, u32[]{:S(2)}) copy-start(pred[24]{0:T(512)(128)(4,1)S(1)} %get-tuple-element.252) | copy-start | bytes 76
  18.1 164.8 %copy-start.111 = (pred[24]{0:T(512)(128)(4,1)}, pred[24]{0:T(512)(128)(4,1)S(1)}, u32[]{:S(2)}) copy-start(pred[24]{0:T(512)(128)(4,1)S(1)} %get-tuple-element.253) | copy-start | bytes 76
  18.1 164.8 %copy-start.114 = (pred[24]{0:T(512)(128)(4,1)}, pred[24]{0:T(512)(128)(4,1)S(1)}, u32[]{:S(2)}) copy-start(pred[24]{0:T(512)(128)(4,1)S(1)} %get-tuple-element.254) | copy-start | bytes 76
  18.1 164.8 %copy-start.117 = (pred[24]{0:T(512)(128)(4,1)}, pred[24]{0:T(512)(128)(4,1)S(1)}, u32[]{:S(2)}) copy-start(pred[24]{0:T(512)(128)(4,1)S(1)} %get-tuple-element.255) | copy-start | bytes 76
  18.1 164.8 %copy-start.119 = (pred[24]{0:T(512)(128)(4,1)}, pred[24]{0:T(512)(128)(4,1)S(1)}, u32[]{:S(2)}) copy-start(pred[24]{0:T(512)(128)(4,1)S(1)} %get-tuple-element.256) | copy-start | bytes 76
  99.0 41.3 %copy-start.202 = (f32[32]{0:T(128)}, f32[32]{0:T(128)S(1)}, u32[]{:S(2)}) copy-start(f32[32]{0:T(128)S(1)} %pad.78.clone) | copy-start | bytes 388
  116.1 23.2 %collective-permute-start.4 = (f32[24,6,256]{2,0,1:T(8,128)}, f32[24,6,256]{2,0,1:T(8,128)}, u32[]{:S(2)}, u32[]{:S(2)}) collective-permute-start(f32[24,6,256]{2,0,1:T(8,128)} %constant_dynamic-update-slice_fusion.12), channel_id=1, source_target_pairs={{0,1},{1,2},{2,3},{3,4},{4,5},{5,6},{6,7},{7,8},{8,9},{9,10},{10,1... | collective-permute-start | bytes 442376 | tf_op jit(solution)/shard_map/ppermute | solution.py:21
  118.0 22.5 %collective-permute-start.5 = (f32[24,6,256]{2,0,1:T(8,128)}, f32[24,6,256]{2,0,1:T(8,128)S(1)}, u32[]{:S(2)}, u32[]{:S(2)}) collective-permute-start(f32[24,6,256]{2,0,1:T(8,128)} %constant_dynamic-update-slice_fusion.12), channel_id=1, source_target_pairs={{1,0},{2,1},{3,2},{4,3},{5,4},{6,5},{7,6},{8,7},{9,8},{10,9},{11,1... | collective-permute-start | bytes 442376 | tf_op jit(solution)/shard_map/ppermute | solution.py:21
  125.9 14.3 %collective-permute-start.2 = (f32[24,6,256]{2,0,1:T(8,128)S(1)}, f32[24,6,256]{2,0,1:T(8,128)S(1)}, u32[]{:S(2)}, u32[]{:S(2)}) collective-permute-start(f32[24,6,256]{2,0,1:T(8,128)S(1)} %constant_dynamic-update-slice_fusion), channel_id=1, source_target_pairs={{0,1},{1,2},{2,3},{3,4},{4,5},{5,6},{6,7},{7,8},{8,9},{9,10},{10,1... | collective-permute-start | bytes 442376 | tf_op jit(solution)/shard_map/ppermute | solution.py:21
  127.8 13.8 %collective-permute-start.3 = (f32[24,6,256]{2,0,1:T(8,128)S(1)}, f32[24,6,256]{2,0,1:T(8,128)S(1)}, u32[]{:S(2)}, u32[]{:S(2)}) collective-permute-start(f32[24,6,256]{2,0,1:T(8,128)S(1)} %constant_dynamic-update-slice_fusion), channel_id=1, source_target_pairs={{1,0},{2,1},{3,2},{4,3},{5,4},{6,5},{7,6},{8,7},{9,8},{10,9},{11,1... | collective-permute-start | bytes 442376 | tf_op jit(solution)/shard_map/ppermute | solution.py:21
  190.2 24.7 %copy-start.4 = (f32[24,16,256]{2,0,1:T(8,128)}, f32[24,16,256]{2,0,1:T(8,128)S(1)}, u32[]{:S(2)}) copy-start(f32[24,16,256]{2,0,1:T(8,128)S(1)} %get-tuple-element.13) | copy-start | bytes 1179652
  198.9 37.8 %collective-permute-start.6 = (f32[24,6,256]{2,0,1:T(8,128)}, f32[24,6,256]{2,0,1:T(8,128)}, u32[]{:S(2)}, u32[]{:S(2)}) collective-permute-start(f32[24,6,256]{2,0,1:T(8,128)} %constant_dynamic-update-slice_fusion.18), channel_id=1, source_target_pairs={{0,1},{1,2},{2,3},{3,4},{4,5},{5,6},{6,7},{7,8},{8,9},{9,10},{10,1... | collective-permute-start | bytes 442376 | tf_op jit(solution)/shard_map/ppermute | solution.py:21
  200.8 36.9 %collective-permute-start.7 = (f32[24,6,256]{2,0,1:T(8,128)}, f32[24,6,256]{2,0,1:T(8,128)}, u32[]{:S(2)}, u32[]{:S(2)}) collective-permute-start(f32[24,6,256]{2,0,1:T(8,128)} %constant_dynamic-update-slice_fusion.18), channel_id=1, source_target_pairs={{1,0},{2,1},{3,2},{4,3},{5,4},{6,5},{7,6},{8,7},{9,8},{10,9},{11,1... | collective-permute-start | bytes 442376 | tf_op jit(solution)/shard_map/ppermute | solution.py:21
  317.0 12.2 %collective-permute-start.8 = (f32[24,6,256]{2,0,1:T(8,128)}, f32[24,6,256]{2,0,1:T(8,128)S(1)}, u32[]{:S(2)}, u32[]{:S(2)}) collective-permute-start(f32[24,6,256]{2,0,1:T(8,128)} %constant_dynamic-update-slice_fusion.24), channel_id=1, source_target_pairs={{0,1},{1,2},{2,3},{3,4},{4,5},{5,6},{6,7},{7,8},{8,9},{9,10},{10,1... | collective-permute-start | bytes 442376 | tf_op jit(solution)/shard_map/ppermute | solution.py:21
  320.3 9.0 %collective-permute-start.9 = (f32[24,6,256]{2,0,1:T(8,128)}, f32[24,6,256]{2,0,1:T(8,128)S(1)}, u32[]{:S(2)}, u32[]{:S(2)}) collective-permute-start(f32[24,6,256]{2,0,1:T(8,128)} %constant_dynamic-update-slice_fusion.24), channel_id=1, source_target_pairs={{1,0},{2,1},{3,2},{4,3},{5,4},{6,5},{7,6},{8,7},{9,8},{10,9},{11,1... | collective-permute-start | bytes 442376 | tf_op jit(solution)/shard_map/ppermute | solution.py:21
  398.0 49.8 %copy-start.208 = (f32[4]{0:T(128)S(1)}, f32[4]{0:T(128)}, u32[]{:S(2)}) copy-start(f32[4]{0:T(128)} %copy-done.207) | copy-start | bytes 52
  447.9 19.8 %collective-permute-start.10 = (f32[4]{0:T(128)S(1)}, f32[4]{0:T(128)S(1)}, u32[]{:S(2)}, u32[]{:S(2)}) collective-permute-start(f32[4]{0:T(128)S(1)} %dynamic_slice.76), channel_id=1, source_target_pairs={{0,16},{16,32},{32,48},{48,64},{64,80},{80,96},{96,112},{1,17},{17... | collective-permute-start | bytes 56 | tf_op jit(solution)/shard_map/ppermute | solution.py:21
  468.1 4.8 collective-permute-start.11
  545.9 3.0 collective-permute-start.12
  549.1 5.0 collective-permute-start.13
  626.9 3.0 collective-permute-start.14
  630.1 5.0 collective-permute-start.15
  711.8 11.9 %collective-permute-start.16 = (f32[24,6,256]{2,0,1:T(8,128)S(1)}, f32[24,6,256]{2,0,1:T(8,128)S(1)}, u32[]{:S(2)}, u32[]{:S(2)}) collective-permute-start(f32[24,6,256]{2,0,1:T(8,128)S(1)} %constant_dynamic-update-slice_fusion.30), channel_id=1, source_target_pairs={{0,1},{1,2},{2,3},{3,4},{4,5},{5,6},{6,7},{7,8},{8,9},{9,10},{10,1... | collective-permute-start | bytes 442376 | tf_op jit(solution)/shard_map/ppermute | solution.py:21
  713.7 10.1 %collective-permute-start.17 = (f32[24,6,256]{2,0,1:T(8,128)S(1)}, f32[24,6,256]{2,0,1:T(8,128)S(1)}, u32[]{:S(2)}, u32[]{:S(2)}) collective-permute-start(f32[24,6,256]{2,0,1:T(8,128)S(1)} %constant_dynamic-update-slice_fusion.30), channel_id=1, source_target_pairs={{1,0},{2,1},{3,2},{4,3},{5,4},{6,5},{7,6},{8,7},{9,8},{10,9},{11,1... | collective-permute-start | bytes 442376 | tf_op jit(solution)/shard_map/ppermute | solution.py:21
  772.1 11.9 %collective-permute-start.18 = (f32[24,6,256]{2,0,1:T(8,128)}, f32[24,6,256]{2,0,1:T(8,128)S(1)}, u32[]{:S(2)}, u32[]{:S(2)}) collective-permute-start(f32[24,6,256]{2,0,1:T(8,128)} %constant_dynamic-update-slice_fusion.36), channel_id=1, source_target_pairs={{0,1},{1,2},{2,3},{3,4},{4,5},{5,6},{6,7},{7,8},{8,9},{9,10},{10,1... | collective-permute-start | bytes 442376 | tf_op jit(solution)/shard_map/ppermute | solution.py:21
  774.0 10.1 %collective-permute-start.19 = (f32[24,6,256]{2,0,1:T(8,128)}, f32[24,6,256]{2,0,1:T(8,128)S(1)}, u32[]{:S(2)}, u32[]{:S(2)}) collective-permute-start(f32[24,6,256]{2,0,1:T(8,128)} %constant_dynamic-update-slice_fusion.36), channel_id=1, source_target_pairs={{1,0},{2,1},{3,2},{4,3},{5,4},{6,5},{7,6},{8,7},{9,8},{10,9},{11,1... | collective-permute-start | bytes 442376 | tf_op jit(solution)/shard_map/ppermute | solution.py:21
  (204 other events, 723.3 us)
where the time goes:
time: 851 us; the launch traced here: 838 us
  local copies, waits for them, and re-layouts  579 us (68%)
  starting transfers between devices  82.4 us (10%)
  other arithmetic  77.9 us (9%)
  blocking collectives  71.1 us (8%)
  between operations  19.4 us (2%)
  waiting for transfers between devices  9.14 us (1%)
    gather x12, local copies, waits for them, and re-layouts, local(): current[positions]  278 us
    squeeze x160, local copies, waits for them, and re-layouts, gather_ghosts(): candidate = extended[LAYER + step_k:LAYER + step_k + slots_n, source_face]  142 us
    ppermute x20, starting transfers between devices, passed_along(): return lax.ppermute(shard, axis, pairs)  82.4 us
    unnamed x1, blocking collectives  42.2 us
    select_n x26, other arithmetic, gather_ghosts(): jnp.where((relative[face_index] == step_k)[:, None], candidate, gathered)  39.5 us
    reshape x6, local copies, waits for them, and re-layouts, beside(): jnp.repeat(ghosts[:, 5].reshape(slots_here, block_edge, block_edge), bloc...  21.2 us
    reshape x6, local copies, waits for them, and re-layouts, beside(): jnp.repeat(ghosts[:, 4].reshape(slots_here, block_edge, block_edge), bloc...  20.3 us
  transfers between devices with their start and end apart: 20, of which 5 were waited for; matrix products, arithmetic and copies ran while one was open for 13% of the time, Pallas kernels for 0%

commit v1 on v0

v1 whole, which is shorter than its diff:
```python
import functools

import jax
import jax.numpy as jnp
from jax import lax
from jax.experimental import pallas as pl
from jax.experimental.pallas import tpu as pltpu
from jax.sharding import PartitionSpec as P

BE = 16
BLK = 16
CAP = 24
LN = 128
RELAX_FINE = 0.8
RELAX_COARSE = 0.7
MESH = pl.DeviceIdType.MESH
F32 = jnp.float32
I32 = jnp.int32
GROUP = (0, 0, 1, 1, 2, 2, 3, 3, 4, 4, 4, 4)
SOURCE = (2, 3, 0, 1, 6, 7, 4, 5)
X_MU, X_U0, X_U1, X_W1, X_U2, X_V1 = range(6)
N_X = 6


def chunk(h):
    return slice(h * LN, (h + 1) * LN)


def steps(n, body, init=None):
    if init is None:
        lax.fori_loop(0, n, lambda i, _: (body(i), 0)[1], 0, unroll=n)
        return None
    return lax.fori_loop(0, n, body, init, unroll=n)


def kernel(
    n_grp, n_sub, nblk,
    pot, rs, mu, owner, neigh, out,
    mu_v, u0_v, rs_v, own_v, nb_v, out_v,
    u, w, cx, cy, cz, dint, t0, inv, coef, rhs, gx, gy, gz, base, base_w,
    own_f, src_f, mu_f, own_mu, ghost, ghost_w, cface, pface, src_w,
    rel, route, bnd, col, qmat, link_w, share_w, corr, rsum,
    send, recv, total, group_total, tail_send, tail_recv, window,
    in_sem, out_sem, x_send, x_recv, l_send, l_recv, s_send, s_recv,
    a_send, a_recv, b_send, b_recv, t_send, t_recv,
):
    grp, sub = lax.axis_index("grp"), lax.axis_index("sub")
    devices = n_grp * n_sub
    me = grp * n_sub + sub

    def dev(by):
        other = lax.rem(me + by + devices, devices)
        return (lax.div(other, n_sub), lax.rem(other, n_sub))

    def in_group(by):
        return (grp, lax.rem(sub + by + n_sub, n_sub))

    def across(by):
        return (lax.rem(grp + by + n_grp, n_grp), sub)

    loads = [
        pltpu.make_async_copy(a, b, in_sem.at[i])
        for i, (a, b) in enumerate(
            ((mu, mu_v), (neigh, nb_v), (pot, u0_v), (rs, rs_v), (owner, own_v))
        )
    ]
    for copy in loads:
        copy.start()

    barrier = pltpu.get_barrier_semaphore()
    for by in (1, -1, 2, -2):
        pl.semaphore_signal(barrier, inc=1, device_id=dev(by), device_id_type=MESH)
    for by in range(1, n_sub):
        pl.semaphore_signal(barrier, inc=1, device_id=in_group(by), device_id_type=MESH)
    for by in range(1, n_grp):
        pl.semaphore_signal(barrier, inc=1, device_id=across(by), device_id_type=MESH)

    lane = lax.broadcasted_iota(I32, (BLK, LN), 1)
    xpos = lane & 15
    yrow = lane >> 4
    row = lax.broadcasted_iota(I32, (BLK, LN), 0)
    lane8 = lax.broadcasted_iota(I32, (8, LN), 1)
    row8 = lax.broadcasted_iota(I32, (8, LN), 0)
    x_first, x_last = xpos == 0, xpos == BE - 1
    x_face = x_first | x_last
    y_first, y_last = lane < BE, lane >= LN - BE
    even = (lane & 1) == 0
    zero = jnp.zeros((BLK, LN), F32)

    def turn(v, by):
        if isinstance(by, int):
            by = by % LN
            return v if by == 0 else pltpu.roll(v, by, 1)
        return pltpu.roll(v, by & (LN - 1), 1)

    def lower_y(v0, v1):
        a, b = turn(v0, BE), turn(v1, BE)
        return a, jnp.where(y_first, a, b)

    def upper_y(v0, v1):
        a, b = turn(v0, -BE), turn(v1, -BE)
        return jnp.where(y_last, b, a), b

    def faces_of(produce, faces_ref, plane):
        for zg in range(2):
            def body(i, carry, zg=zg):
                x0, x1, y2, y3 = carry
                v0, v1 = produce(zg, i)
                here = (xpos == 2 * i) | (xpos == ((2 * i + 15) & 15))
                x0 = jnp.where(here, turn(v0, 2 * i), x0)
                x1 = jnp.where(here, turn(v1, 2 * i), x1)
                line = yrow == i
                y2 = jnp.where(line, turn(v0, BE * i), y2)
                y3 = jnp.where(line, turn(v1, BE * i + BE), y3)
                return x0, x1, y2, y3

            x0, x1, y2, y3 = steps(8, body, (zero, zero, zero, zero))
            faces_ref[8 + 2 * zg] = x0
            faces_ref[9 + 2 * zg] = x1
            faces_ref[4 + zg] = y2
            faces_ref[6 + zg] = y3
        for h in range(2):
            faces_ref[h] = plane(0, h)
            faces_ref[2 + h] = plane(BE - 1, h)

    def sources(faces_ref, src_ref):
        for k in range(12):
            if k < 8:
                v = faces_ref[SOURCE[k]]
            else:
                x = faces_ref[k]
                v = jnp.where(even, turn(x, -15), turn(x, 15))
            src_ref[k, 8:24, :] = v

    def send_faces(src_ref, slot):
        for m in range(6):
            pair = []
            for k in (2 * m, 2 * m + 1):
                edge = jnp.where(row8 < 4, src_ref[k, 8:16, :], src_ref[k, 16:24, :])
                way = route[GROUP[k]]
                d = jnp.zeros((8, LN), F32)
                for r in (4,) if k < 4 else range(1, 8):
                    d = jnp.where(way == r, pltpu.roll(edge, r, 0), d)
                pair.append(d)
            d0, d1 = pair
            send[slot, 0, m] = jnp.where(row8 < 4, d0, pltpu.roll(d1, 4, 0))
            send[slot, 1, m] = jnp.where(row8 < 4, pltpu.roll(d0, 4, 0), d1)
        for copy in face_copies(slot):
            copy.start()

    def face_copies(slot):
        return [
            pltpu.make_async_remote_copy(
                src_ref=send.at[slot, way],
                dst_ref=recv.at[slot, way],
                send_sem=x_send.at[slot, way],
                recv_sem=x_recv.at[slot, way],
                device_id=dev(1 - 2 * way),
                device_id_type=MESH,
            )
            for way in range(2)
        ]

    def local_ghosts(src_ref, ghost_ref):
        for k in range(12):
            r = rel[GROUP[k]]
            g = zero
            for by in (-4, 4) if k < 4 else range(-4, 5):
                g = jnp.where(r == by, src_ref[k, 8 + by : 24 + by, :], g)
            ghost_ref[k] = g

    def add_remote(slot, ghost_ref):
        for copy in face_copies(slot):
            copy.wait_recv()
        for m in range(6):
            lo, hi = recv[slot, 0, m], recv[slot, 1, m]
            lo1, hi0 = pltpu.roll(lo, 4, 0), pltpu.roll(hi, 4, 0)
            ghost_ref[2 * m, 0:8, :] += jnp.where(row8 < 4, lo, 0.0)
            ghost_ref[2 * m + 1, 0:8, :] += jnp.where(row8 < 4, lo1, 0.0)
            ghost_ref[2 * m, 8:16, :] += jnp.where(row8 < 4, 0.0, hi0)
            ghost_ref[2 * m + 1, 8:16, :] += jnp.where(row8 < 4, 0.0, hi)

    def spread_x(faces_ref, zg, i, h):
        return turn(faces_ref[8 + 2 * zg + h], LN - 2 * i)

    def spread_y(faces_ref, zg, i, h):
        return turn(faces_ref[(4, 6)[h] + zg], LN - BE * i - (0, BE)[h])

    first = BLK * me - 24
    loads[1].wait()
    low = lax.div(first + LN, LN) - 1
    shift = first - low * LN
    tiles = nblk // LN

    def table(k):
        at = pl.multiple_of(lax.rem(k + tiles, tiles) * LN, LN)
        rows6 = nb_v[:, pl.ds(at, LN)]
        return jnp.concatenate([rows6, jnp.full((2, LN), -1, I32)], axis=0)

    back = LN - shift
    ta, tb = turn(table(low), back), turn(table(low + 1), back)
    ids = first + lane8
    nb = jnp.where(lane8 < back, ta, tb)
    nb = jnp.where((nb >= 0) & (ids >= 0) & (ids < nblk), nb - first, -1000).astype(F32)
    nbt = nb.T
    col[...] = nbt

    def columns(f, lo, n):
        return jnp.broadcast_to(col[lo : lo + n, f : f + 1], (n, LN))

    rowf = row.astype(F32)
    row8f = row8.astype(F32)
    rels, routes, bnds = [], [], []
    for f in range(6):
        to = columns(f, 24, 16)
        near = (to >= 24.0) & (to < 40.0)
        rels.append(jnp.where(near, to - 24.0 - rowf, 99.0))
        bnds.append(jnp.where(to < 0.0, 1.0, 0.0))
        to8 = jnp.where(row8 < 4, columns(f, 40, 8), columns(f, 16, 8))
        j = jnp.where(row8 < 4, to8 - 32.0, to8 - 24.0)
        ok = jnp.where(row8 < 4, jnp.where(j >= 4.0, 1.0, 0.0), jnp.where(j >= 0.0, 1.0, 0.0))
        ok = ok * jnp.where(row8 < 4, jnp.where(j < 8.0, 1.0, 0.0), jnp.where(j < 4.0, 1.0, 0.0))
        r = row8f - j
        routes.append(jnp.where(ok > 0.5, jnp.where(r < 0.0, r + 8.0, r), 99.0))
    even8 = (lane8 & 1) == 0
    for g in range(4):
        rel[g], route[g], bnd[g] = rels[g], routes[g], bnds[g]
    rel[4] = jnp.where(even, rels[4], rels[5])
    bnd[4] = jnp.where(even, bnds[4], bnds[5])
    route[4] = jnp.where(even8, routes[4], routes[5])

    def plane_of(ref):
        return lambda z, h: ref[:, z * 256 + h * LN : z * 256 + (h + 1) * LN]

    def from_input(ref, store=None):
        def produce(zg, i):
            at = pl.multiple_of((zg * 8 + i) * 256, 256)
            v0, v1 = ref[:, pl.ds(at, LN)], ref[:, pl.ds(at + LN, LN)]
            if store is not None:
                store[zg * 8 + i + 1, :, chunk(0)] = v0
                store[zg * 8 + i + 1, :, chunk(1)] = v1
            return v0, v1

        return produce

    loads[0].wait()
    faces_of(from_input(mu_v), own_mu, plane_of(mu_v))
    sources(own_mu, src_w)
    pl.semaphore_wait(barrier, 4 + n_sub - 1 + n_grp - 1)
    send_faces(src_w, X_MU)
    loads[2].wait()
    faces_of(from_input(u0_v, u), own_f, plane_of(u0_v))
    sources(own_f, src_f)
    send_faces(src_f, X_U0)

    local_ghosts(src_w, mu_f)
    local_ghosts(src_f, ghost)
    for ref in (u, w):
        ref[0] = jnp.zeros((BLK, 256), F32)
        ref[BE + 1] = jnp.zeros((BLK, 256), F32)
    cz[0] = jnp.zeros((BLK, 256), F32)
    cz[BE] = jnp.zeros((BLK, 256), F32)

    def mean(a, b):
        return 2.0 * a * b / (a + b)

    def inner_couplings(z):
        at = pl.multiple_of(z * 256, 256)
        m0, m1 = mu_v[:, pl.ds(at, LN)], mu_v[:, pl.ds(at + LN, LN)]
        y0, y1 = lower_y(m0, m1)
        cx[z, :, chunk(0)] = jnp.where(x_first, 0.0, mean(m0, turn(m0, 1)))
        cx[z, :, chunk(1)] = jnp.where(x_first, 0.0, mean(m1, turn(m1, 1)))
        cy[z, :, chunk(0)] = jnp.where(y_first, 0.0, mean(m0, y0))
        cy[z, :, chunk(1)] = mean(m1, y1)

    def z_couplings(z):
        at = pl.multiple_of(z * 256, 256)
        a = mu_v[:, pl.ds(at, 256)]
        b = mu_v[:, pl.ds(at + 256, 256)]
        cz[z + 1] = mean(a, b)

    steps(BE, inner_couplings)
    steps(BE - 1, z_couplings)
    loads[3].wait()

    def around(z):
        cx0, cx1 = cx[z, :, chunk(0)], cx[z, :, chunk(1)]
        cy0, cy1 = cy[z, :, chunk(0)], cy[z, :, chunk(1)]
        uy0, uy1 = upper_y(cy0, cy1)
        uy1 = jnp.where(y_last, 0.0, uy1)
        lo = (cz[z, :, chunk(0)], cz[z, :, chunk(1)])
        up = (cz[z + 1, :, chunk(0)], cz[z + 1, :, chunk(1)])
        return (
            (lo[0], up[0], cy0, uy0, cx0, turn(cx0, -1)),
            (lo[1], up[1], cy1, uy1, cx1, turn(cx1, -1)),
        )

    def beside(ref, z):
        v0, v1 = ref[z + 1, :, chunk(0)], ref[z + 1, :, chunk(1)]
        l0, l1 = lower_y(v0, v1)
        p0, p1 = upper_y(v0, v1)
        return (v0, v1), (
            (ref[z, :, chunk(0)], ref[z + 2, :, chunk(0)], l0, p0, turn(v0, 1), turn(v0, -1)),
            (ref[z, :, chunk(1)], ref[z + 2, :, chunk(1)], l1, p1, turn(v1, 1), turn(v1, -1)),
        )

    def first_terms(z, acc):
        c = around(z)
        _, n = beside(u, z)
        for h in range(2):
            at = pl.multiple_of(z * 256 + h * LN, LN)
            r = rs_v[:, pl.ds(at, LN)]
            d = c[h][0]
            t = r + c[h][0] * n[h][0]
            for f in range(1, 6):
                d = d + c[h][f]
                t = t + c[h][f] * n[h][f]
            dint[z, :, chunk(h)] = d
            t0[z, :, chunk(h)] = t
            acc = acc + r
        return acc

    acc = steps(BE, first_terms, zero)
    rsum[...] = jnp.broadcast_to(jnp.sum(acc, axis=1, keepdims=True), (BLK, LN))

    add_remote(X_MU, mu_f)
    for k in range(12):
        m = own_mu[k]
        g = jnp.where(bnd[GROUP[k]] > 0.5, m, mu_f[k])
        cface[k] = mean(m, g)
    for h in range(2):
        dint[0, :, chunk(h)] += cface[h]
        dint[BE - 1, :, chunk(h)] += cface[2 + h]
    add_remote(X_U0, ghost)
    for k in range(12):
        pface[k] = cface[k] * ghost[k]
    for h in range(2):
        t0[0, :, chunk(h)] += pface[h]
        t0[BE - 1, :, chunk(h)] += pface[2 + h]

    y_face = (y_first, y_last)

    def sweep_first(zg, i):
        z = zg * 8 + i
        vs = []
        for h in range(2):
            d = dint[z, :, chunk(h)]
            t = t0[z, :, chunk(h)]
            d = d + jnp.where(x_face, spread_x(cface, zg, i, h), 0.0)
            d = d + jnp.where(y_face[h], spread_y(cface, zg, i, h), 0.0)
            t = t + jnp.where(x_face, spread_x(pface, zg, i, h), 0.0)
            t = t + jnp.where(y_face[h], spread_y(pface, zg, i, h), 0.0)
            q = RELAX_FINE / d
            inv[z, :, chunk(h)] = q
            v = (1.0 - RELAX_FINE) * u[z + 1, :, chunk(h)] + q * t
            u[z + 1, :, chunk(h)] = v
            vs.append(v)
        return vs

    def plane_u(ref):
        return lambda z, h: ref[z + 1, :, chunk(h)]

    faces_of(sweep_first, own_f, plane_u(u))
    sources(own_f, src_f)
    send_faces(src_f, X_U1)

    bx = jnp.where(x_first, bnds[4], jnp.where(x_last, bnds[5], 0.0))
    by_ = (jnp.where(y_first, bnd[2], 0.0), jnp.where(y_last, bnd[3], 0.0))

    for h in range(2):
        gz[0, :, chunk(h)] = cface[h] * inv[0, :, chunk(h)]
        gz[1, :, chunk(h)] = cface[2 + h] * inv[BE - 1, :, chunk(h)]

    def coefficients(zg, i):
        z = zg * 8 + i
        c = around(z)
        vs = []
        for h in range(2):
            q = inv[z, :, chunk(h)]
            for f in range(6):
                coef[f, z, :, chunk(h)] = c[h][f] * q
            at = pl.multiple_of(z * 256 + h * LN, LN)
            rhs[z, :, chunk(h)] = rs_v[:, pl.ds(at, LN)] * q
            fx = jnp.where(x_face, spread_x(cface, zg, i, h), 0.0) * q
            fy = jnp.where(y_face[h], spread_y(cface, zg, i, h), 0.0) * q
            gx[z, :, chunk(h)] = fx
            gy[z, :, chunk(h)] = fy
            v = 1.0 - fx * bx - fy * by_[h]
            w[z + 1, :, chunk(h)] = v
            vs.append(v)
        return vs

    for zg in range(2):
        steps(8, lambda i, zg=zg: (coefficients(zg, i), None)[1])

    def inner_sweep(ref, base_ref, with_rhs):
        def body(z):
            v, n = beside(ref, z)
            for h in range(2):
                b = (1.0 - RELAX_FINE) * v[h]
                if with_rhs:
                    b = b + rhs[z, :, chunk(h)]
                for f in range(6):
                    b = b + coef[f, z, :, chunk(h)] * n[h][f]
                base_ref[z, :, chunk(h)] = b

        steps(BE, body)

    def add_z(ghost_ref, base_ref):
        for h in range(2):
            base_ref[0, :, chunk(h)] += gz[0, :, chunk(h)] * ghost_ref[h]
            base_ref[BE - 1, :, chunk(h)] += gz[1, :, chunk(h)] * ghost_ref[2 + h]

    def outer_sweep(ghost_ref, base_ref, ref):
        def produce(zg, i):
            z = zg * 8 + i
            vs = []
            for h in range(2):
                v = base_ref[z, :, chunk(h)]
                v = v + gx[z, :, chunk(h)] * spread_x(ghost_ref, zg, i, h)
                v = v + gy[z, :, chunk(h)] * spread_y(ghost_ref, zg, i, h)
                ref[z + 1, :, chunk(h)] = v
                vs.append(v)
            return vs

        return produce

    inner_sweep(u, base, True)
    local_ghosts(src_f, ghost)

    def face_sums(value):
        sums = []
        for f in range(4):
            s = value(2 * f) + value(2 * f + 1)
            sums.append(jnp.sum(s, axis=1, keepdims=True))
        s = value(8) + value(9) + value(10) + value(11)
        sums.append(jnp.sum(jnp.where(even, s, 0.0), axis=1, keepdims=True))
        sums.append(jnp.sum(jnp.where(even, 0.0, s), axis=1, keepdims=True))
        return sums

    links = face_sums(lambda k: cface[k])
    tile = zero
    link_total = links[0]
    for f in range(6):
        tile = jnp.where(lane == f, links[f], tile)
        if f:
            link_total = link_total + links[f]
    link_w[24:40] = tile
    link_w[0:8] = jnp.ones((8, LN), F32)
    link_w[56:64] = jnp.ones((8, LN), F32)

    def remote(src, dst, a, b, to):
        return pltpu.make_async_remote_copy(
            src_ref=src, dst_ref=dst, send_sem=a, recv_sem=b, device_id=to, device_id_type=MESH
        )

    def two_way(ref, a, b):
        return [
            remote(ref.at[pl.ds(24, 16)], ref.at[pl.ds(8, 16)], a.at[0], b.at[0], dev(1)),
            remote(ref.at[pl.ds(24, 16)], ref.at[pl.ds(40, 16)], a.at[1], b.at[1], dev(-1)),
        ]

    link_copies = two_way(link_w, l_send, l_recv)
    for copy in link_copies:
        copy.start()

    for h in range(2):
        w[1, :, chunk(h)] -= gz[0, :, chunk(h)] * bnd[0]
        w[BE, :, chunk(h)] -= gz[1, :, chunk(h)] * bnd[1]

    def from_w(zg, i):
        z = zg * 8 + i
        return w[z + 1, :, chunk(0)], w[z + 1, :, chunk(1)]

    faces_of(from_w, own_mu, plane_u(w))
    sources(own_mu, src_w)
    send_faces(src_w, X_W1)

    add_remote(X_U1, ghost)
    add_z(ghost, base)
    faces_of(outer_sweep(ghost, base, u), own_f, plane_u(u))
    sources(own_f, src_f)
    send_faces(src_f, X_U2)

    sums = face_sums(lambda k: cface[k] * own_f[k])
    left = rsum[:, 0:1]
    group_left = left
    tile = zero
    for f in range(6):
        tile = jnp.where(lane == f, sums[f], tile)
        left = left - sums[f]
        group_left = group_left - sums[f] * bnds[f][:, 0:1]
    share_w[24:40] = jnp.where(lane == 6, left, tile)
    share_copies = two_way(share_w, s_send, s_recv) + [
        remote(
            share_w.at[pl.ds(32, 8)], share_w.at[pl.ds(0, 8)], s_send.at[2], s_recv.at[2], dev(2)
        ),
        remote(
            share_w.at[pl.ds(24, 8)], share_w.at[pl.ds(56, 8)], s_send.at[3], s_recv.at[3], dev(-2)
        ),
    ]
    for copy in share_copies:
        copy.start()
    total[0] = jnp.where(
        lane8 < 64,
        jnp.sum(group_left, axis=0, keepdims=True),
        jnp.sum(link_total, axis=0, keepdims=True),
    )
    total_copies = [
        remote(total.at[0], total.at[i], a_send.at[i], a_recv.at[i], in_group(i))
        for i in range(1, n_sub)
    ]
    for copy in total_copies:
        copy.start()

    inner_sweep(u, base, True)
    local_ghosts(src_f, ghost)
    for copy in link_copies:
        copy.wait_recv()
    i64 = lax.broadcasted_iota(I32, (64, 64), 0)
    l64 = lax.broadcasted_iota(I32, (64, 64), 1)
    l64f = l64.astype(F32)
    diagonal = link_w[:, 0:1]
    for f in range(1, 6):
        diagonal = diagonal + link_w[:, f : f + 1]
    gain = RELAX_COARSE / diagonal
    ident = jnp.where(i64 == l64, 1.0, 0.0)
    hot = [jnp.where(col[0:64, f : f + 1] == l64f, 1.0, 0.0) for f in range(6)]
    gmat = link_w[:, 0:1] * hot[0]
    for f in range(1, 6):
        gmat = gmat + link_w[:, f : f + 1] * hot[f]
    gmat = gmat * gain + (1.0 - RELAX_COARSE) * ident

    def product(a, b):
        return lax.dot_general(
            a,
            b,
            (((1,), (0,)), ((), ())),
            precision=lax.Precision.HIGHEST,
            preferred_element_type=F32,
        )

    ymat = ident + gmat
    ymat = ident + product(ymat, gmat)
    ymat = ident + product(ymat, gmat)
    scale = jnp.sum(ident * gain, axis=0, keepdims=True)
    picks = jnp.concatenate([ident[24:40]] + [hot[f][24:40] for f in range(6)], axis=0)
    qmat[...] = product(picks, ymat) * scale

    inner_sweep(w, base_w, False)
    local_ghosts(src_w, ghost_w)
    add_remote(X_W1, ghost_w)
    add_z(ghost_w, base_w)
    finish_w = outer_sweep(ghost_w, base_w, w)
    for zg in range(2):
        steps(8, lambda i, zg=zg: (finish_w(zg, i), None)[1])

    for copy in share_copies:
        copy.wait_recv()
    acc = ident * share_w[:, 6:7]
    i64f = i64.astype(F32)
    for f in range(6):
        acc = acc + jnp.where(nb[f : f + 1, 0:64] == i64f, share_w[:, (f ^ 1) : (f ^ 1) + 1], 0.0)
    source_row = jnp.sum(acc, axis=0, keepdims=True)
    fixed = jnp.sum(qmat[...] * source_row, axis=1, keepdims=True)
    own_fix = fixed[0:16]
    corr[0] = jnp.broadcast_to(own_fix, (BLK, LN))
    for f in range(6):
        corr[1 + f] = jnp.broadcast_to(fixed[16 + 16 * f : 32 + 16 * f] - own_fix, (BLK, LN))
    fix_x = jnp.where(even, corr[5], corr[6])

    add_remote(X_U2, ghost)
    for k in range(12):
        ghost[k] += corr[1 + GROUP[k]] if k < 8 else fix_x
    add_z(ghost, base)
    third = outer_sweep(ghost, base, u)

    def third_sweep(zg, i):
        z = zg * 8 + i
        vs = third(zg, i)
        vs = [vs[h] + corr[0] for h in range(2)]
        for h in range(2):
            u[z + 1, :, chunk(h)] = vs[h]
        return vs

    faces_of(third_sweep, own_f, plane_u(u))
    sources(own_f, src_f)
    send_faces(src_f, X_V1)

    for copy in total_copies:
        copy.wait_recv()
    part = total[0]
    for i in range(1, n_sub):
        part = part + total[i]
    group_total[0] = part
    group_copies = [
        remote(group_total.at[0], group_total.at[i], b_send.at[i], b_recv.at[i], across(i))
        for i in range(1, n_grp)
    ]
    for copy in group_copies:
        copy.start()

    inner_sweep(u, base, True)
    local_ghosts(src_f, ghost)
    for copy in group_copies:
        copy.wait_recv()
    part = group_total[0]
    for i in range(1, n_grp):
        part = part + group_total[i]
    level = part[0:1, 0:1] / part[0:1, 64:65]
    level = jnp.broadcast_to(level, (BLK, LN))

    add_remote(X_V1, ghost)
    add_z(ghost, base)
    tail_copies = []
    for zg in range(2):
        def last_sweep(i, zg=zg):
            z = zg * 8 + i
            vs = []
            for h in range(2):
                v = base[z, :, chunk(h)] + level * w[z + 1, :, chunk(h)]
                v = v + gx[z, :, chunk(h)] * spread_x(ghost, zg, i, h)
                v = v + gy[z, :, chunk(h)] * spread_y(ghost, zg, i, h)
                window[2 * z + h, 8:24, :] = v
                vs.append(v)
            v0, v1 = vs
            tail_send[0, z] = jnp.where(row8 < 4, pltpu.roll(v0[8:16], 4, 0), v1[8:16])
            tail_send[1, z] = jnp.where(row8 < 4, v0[0:8], pltpu.roll(v1[0:8], 4, 0))

        steps(8, last_sweep)
        for way in range(2):
            copy = remote(
                tail_send.at[way, pl.ds(8 * zg, 8)],
                tail_recv.at[way, pl.ds(8 * zg, 8)],
                t_send.at[way, zg],
                t_recv.at[way, zg],
                dev(1 - 2 * way),
            )
            copy.start()
            tail_copies.append(copy)

    loads[4].wait()
    owners = own_v[...]
    starts = jnp.sum(jnp.where(owners < me, 1.0, 0.0)).astype(I32)
    count = jnp.sum(jnp.where(owners == me, 1.0, 0.0)).astype(I32)
    at = jnp.clip(starts - BLK * me + 8, 4, 12)
    row24 = lax.broadcasted_iota(I32, (CAP, LN), 0)
    live = row24 < count
    out_copies = []
    for zg in range(2):
        for copy in tail_copies[2 * zg : 2 * zg + 2]:
            copy.wait_recv()

        def place(i, zg=zg):
            z = zg * 8 + i
            lo, hi = tail_recv[0, z], tail_recv[1, z]
            window[2 * z, 0:8, :] = pltpu.roll(lo, 4, 0)
            window[2 * z + 1, 0:8, :] = lo
            window[2 * z, 24:32, :] = hi
            window[2 * z + 1, 24:32, :] = pltpu.roll(hi, 4, 0)

        steps(8, place)

        def emit(i, zg=zg):
            z = zg * 8 + i
            for h in range(2):
                lanes = pl.ds(pl.multiple_of(z * 256 + h * LN, LN), LN)
                out_v[:, lanes] = jnp.where(live, window[2 * z + h, pl.ds(at, CAP), :], 0.0)

        steps(8, emit)
        half = pl.ds(zg * 2048, 2048)
        copy = pltpu.make_async_copy(out_v.at[:, half], out.at[:, half], out_sem.at[zg])
        copy.start()
        out_copies.append(copy)

    for slot in range(N_X):
        for copy in face_copies(slot):
            copy.wait_send()
    for copy in link_copies + share_copies + total_copies + group_copies + tail_copies:
        copy.wait_send()
    for copy in out_copies:
        copy.wait()


def local(potential, right_side, permeability, new_owner, neighbours):
    n_grp, n_sub = lax.axis_size("grp"), lax.axis_size("sub")
    nblk = new_owner.shape[0]
    vmem = pltpu.VMEM
    plane = (BLK, 256)
    dma = pltpu.SemaphoreType.DMA
    scratch = [
        vmem((BLK, 4096), F32),
        vmem((BLK, 4096), F32),
        vmem((BLK, 4096), F32),
        vmem((nblk // LN, LN), I32),
        vmem((6, nblk), I32),
        vmem((CAP, 4096), F32),
        vmem((BE + 2, *plane), F32),
        vmem((BE + 2, *plane), F32),
        vmem((BE, *plane), F32),
        vmem((BE, *plane), F32),
        vmem((BE + 1, *plane), F32),
        vmem((BE, *plane), F32),
        vmem((BE, *plane), F32),
        vmem((BE, *plane), F32),
        vmem((6, BE, *plane), F32),
        vmem((BE, *plane), F32),
        vmem((BE, *plane), F32),
        vmem((BE, *plane), F32),
        vmem((2, *plane), F32),
        vmem((BE, *plane), F32),
        vmem((BE, *plane), F32),
        vmem((12, BLK, LN), F32),
        vmem((12, 32, LN), F32),
        vmem((12, BLK, LN), F32),
        vmem((12, BLK, LN), F32),
        vmem((12, BLK, LN), F32),
        vmem((12, BLK, LN), F32),
        vmem((12, BLK, LN), F32),
        vmem((12, BLK, LN), F32),
        vmem((12, 32, LN), F32),
        vmem((5, BLK, LN), F32),
        vmem((5, 8, LN), F32),
        vmem((5, BLK, LN), F32),
        vmem((LN, 8), F32),
        vmem((112, 64), F32),
        vmem((64, LN), F32),
        vmem((64, LN), F32),
        vmem((7, BLK, LN), F32),
        vmem((BLK, LN), F32),
        vmem((N_X, 2, 6, 8, LN), F32),
        vmem((N_X, 2, 6, 8, LN), F32),
        vmem((n_sub, 8, LN), F32),
        vmem((n_grp, 8, LN), F32),
        vmem((2, BE, 8, LN), F32),
        vmem((2, BE, 8, LN), F32),
        vmem((32, 40, LN), F32),
        dma((5,)),
        dma((2,)),
        dma((N_X, 2)),
        dma((N_X, 2)),
        dma((2,)),
        dma((2,)),
        dma((4,)),
        dma((4,)),
        dma((n_sub,)),
        dma((n_sub,)),
        dma((n_grp,)),
        dma((n_grp,)),
        dma((2, 2)),
        dma((2, 2)),
    ]
    return pl.pallas_call(
        functools.partial(kernel, n_grp, n_sub, nblk),
        out_shape=jax.ShapeDtypeStruct((CAP, 4096), F32),
        in_specs=[pl.BlockSpec(memory_space=pl.ANY)] * 5,
        out_specs=pl.BlockSpec(memory_space=pl.ANY),
        scratch_shapes=scratch,
        compiler_params=pltpu.CompilerParams(
            collective_id=0, has_side_effects=True, vmem_limit_bytes=32 * 1024 * 1024
        ),
        cost_estimate=pl.CostEstimate(
            flops=8_000_000, bytes_accessed=1_200_000, transcendentals=0
        ),
        name="cycle",
    )(potential, right_side, permeability, new_owner.reshape(nblk // LN, LN), neighbours)


def solution(mesh):
    in_specs = (P(("grp", "sub"), None), P(("grp", "sub"), None), P(("grp", "sub"), None), P(), P())
    out_specs = P(("grp", "sub"), None)
    return jax.shard_map(local, mesh=mesh, in_specs=in_specs, out_specs=out_specs, check_vma=False)
```

time: 851 us -> 43.7 us (0.05); the launches traced: 838 us -> 43.5 us
  local copies, waits for them, and re-layouts: 579 us -> 5.13 us
  starting transfers between devices: 82.4 us -> 0 us
  other arithmetic: 77.9 us -> 0 us
  blocking collectives: 71.1 us -> 0 us
  Pallas kernels: 0 us -> 38.3 us
  between operations: 19.4 us -> 0.01 us
  waiting for transfers between devices: 9.14 us -> 0 us
    gather x14 -> x0, local copies, waits for them, and re-layouts: 279 us -> none  [the longest x12 278 us: local(): current[positions]]
    squeeze x160 -> x0, local copies, waits for them, and re-layouts: 142 us -> none  [gather_ghosts(): candidate = extended[LAYER + step_k:LAYER + step_k + slots_n, source_face]]
    ppermute x20 -> x0, starting transfers between devices: 82.4 us -> none  [passed_along(): return lax.ppermute(shard, axis, pairs)]
    slice x71 -> x0, local copies, waits for them, and re-layouts: 48.7 us -> none  [the longest x13 9.34 us: face_one(): return values[:, :, 0::block_edge].reshape(slots_here, plane_cells)]
    select_n x39 -> x0, other arithmetic: 46 us -> none  [the longest x26 39.5 us: gather_ghosts(): jnp.where((relative[face_index] == step_k)[:, None], candidate, gathered)]
    reshape x13 -> x0, local copies, waits for them, and re-layouts: 42.3 us -> none  [the longest x6 21.2 us: beside(): jnp.repeat(ghosts[:, 5].reshape(slots_here, block_edge, block_edge), bloc...]
    unnamed x1 -> x0, blocking collectives: 42.2 us -> none
    pallas_call x0 -> x1, Pallas kernels: none -> 38.3 us  [local(): pl.pallas_call(functools.partial(kernel, n_grp, n_sub, nblk), out_shape=j...]
  transfers between devices with their start and end apart: 20 -> 0, of which waited for: 5 -> 0; matrix products, arithmetic and copies ran while one was open for 13% -> 0% of each run, Pallas kernels for 0% -> 0%
where the time goes in v1:
time: 43.7 us; the launch traced here: 43.5 us
  Pallas kernels  38.3 us (88%)
  local copies, waits for them, and re-layouts  5.13 us (12%)
    pallas_call x1, Pallas kernels, local(): pl.pallas_call(functools.partial(kernel, n_grp, n_sub, nblk), out_shape=j...  38.3 us
    unnamed x11, local copies, waits for them, and re-layouts  5.13 us

profile of v1, /device:TPU:1, one launch (start us, length us, event | category | flops | bytes accessed | tf_op | source)
XLA Modules:
  0.0 43.5 jit_solution(1498924552381295102)
XLA Ops:
  0.0 0.0 copy-start
  0.0 0.9 %copy-done = f32[16,4096]{1,0:T(8,128)S(1)} copy-done((f32[16,4096]{1,0:T(8,128)S(1)}, f32[16,4096]{1,0:T(8,128)}, u32[]{:S(2)}) %copy-start) | copy-done | bytes 262168
  1.0 0.0 copy-start.1
  1.0 0.9 %copy-done.1 = f32[16,4096]{1,0:T(8,128)S(1)} copy-done((f32[16,4096]{1,0:T(8,128)S(1)}, f32[16,4096]{1,0:T(8,128)}, u32[]{:S(2)}) %copy-start.1) | copy-done | bytes 262168
  1.9 0.0 copy-start.2
  1.9 0.9 %copy-done.2 = f32[16,4096]{1,0:T(8,128)S(1)} copy-done((f32[16,4096]{1,0:T(8,128)S(1)}, f32[16,4096]{1,0:T(8,128)}, u32[]{:S(2)}) %copy-start.2) | copy-done | bytes 262168
  2.9 0.0 copy-start.3
  2.9 0.8 %copy-done.3 = s32[6,2048]{1,0:T(8,128)S(1)} copy-done((s32[6,2048]{1,0:T(8,128)S(1)}, s32[6,2048]{1,0:T(8,128)}, u32[]{:S(2)}) %copy-start.3) | copy-done | bytes 49176
  3.7 0.0 copy-start.4
  3.7 0.7 %copy-done.4 = s32[2048]{0:T(1024)S(1)} copy-done((s32[2048]{0:T(1024)S(1)}, s32[2048]{0:T(1024)}, u32[]{:S(2)}) %copy-start.4) | copy-done | bytes 8216
  4.4 38.3 %cycle.1 = f32[24,4096]{1,0:T(8,128)S(1)} custom-call(f32[16,4096]{1,0:T(8,128)S(1)} %copy-done, f32[16,4096]{1,0:T(8,128)S(1)} %copy-done.1, f32[16,4096]{1,0:T(8,128)S(1)} %copy-done.2, s32[16,128]{1,0:T(8,128)S(1)} %bitcast.1, s32[6,2048]{1,0:T(8,128)S(1)} %copy-done.3), custom_call_target="tpu_custom_call" | custom-call | flops 8000000 | bytes 1200000 | tf_op jit(solution)/shard_map/cycle/pallas_call | solution.py:753
  42.7 0.7 %copy.7 = f32[24,4096]{1,0:T(8,128)} copy(f32[24,4096]{1,0:T(8,128)S(1)} %cycle.1) | data formatting | bytes 786432
Async XLA Ops:
  0.0 0.9 %copy-start = (f32[16,4096]{1,0:T(8,128)S(1)}, f32[16,4096]{1,0:T(8,128)}, u32[]{:S(2)}) copy-start(f32[16,4096]{1,0:T(8,128)} %pot.1) | copy-start | bytes 786436
  1.0 0.9 %copy-start.1 = (f32[16,4096]{1,0:T(8,128)S(1)}, f32[16,4096]{1,0:T(8,128)}, u32[]{:S(2)}) copy-start(f32[16,4096]{1,0:T(8,128)} %rs.1) | copy-start | bytes 786436
  1.9 0.9 %copy-start.2 = (f32[16,4096]{1,0:T(8,128)S(1)}, f32[16,4096]{1,0:T(8,128)}, u32[]{:S(2)}) copy-start(f32[16,4096]{1,0:T(8,128)} %mu.1) | copy-start | bytes 786436
  2.9 0.8 %copy-start.3 = (s32[6,2048]{1,0:T(8,128)S(1)}, s32[6,2048]{1,0:T(8,128)}, u32[]{:S(2)}) copy-start(s32[6,2048]{1,0:T(8,128)} %neigh.1) | copy-start | bytes 147460
  3.7 0.7 %copy-start.4 = (s32[2048]{0:T(1024)S(1)}, s32[2048]{0:T(1024)}, u32[]{:S(2)}) copy-start(s32[2048]{0:T(1024)} %param.8) | copy-start | bytes 24580

commit v2 on v1

v2 whole, which is shorter than its diff:
```python
import functools
import types

import jax
import jax.numpy as jnp
from jax import lax
from jax.experimental import pallas as pl
from jax.experimental.pallas import tpu as pltpu
from jax.sharding import PartitionSpec as P

BE = 16
BLK = 16
CAP = 24
LN = 128
RELAX_FINE = 0.8
RELAX_COARSE = 0.7
MESH = pl.DeviceIdType.MESH
F32 = jnp.float32
I32 = jnp.int32
GROUP = (0, 0, 1, 1, 2, 2, 3, 3, 4, 4, 4, 4)
SOURCE = (2, 3, 0, 1, 6, 7, 4, 5)
X_MU, X_U0, X_U1, X_U2 = range(4)
N_X = 4
WIN = 80
MINE = 32


def chunk(h):
    return slice(h * LN, (h + 1) * LN)


def steps(n, body, init=None):
    if init is None:
        lax.fori_loop(0, n, lambda i, _: (body(i), 0)[1], 0, unroll=n)
        return None
    return lax.fori_loop(0, n, body, init, unroll=n)


def kernel(
    n_grp, n_sub, nblk,
    pot, rs, mu, owner, neigh, out,
    mu_s, u0_s, rs_s, own_v, nb_v,
    u_s, w_s, cx_s, cy_s, cz_s, dint_s, t0_s, inv_s, coef_s, rhs_s, gx_s, gy_s, gz_s, base_s, base_w_s,
    faces_s, wfaces_s, ghost_s, cface_s, rel_s, bnd_s, corr_s,
    pface, mu_f, own_mu, src_f, src_w, near_local, near_far, keep,
    rel_local, route, col, qmat, link_w, share_w, rsum,
    send, recv, total, group_total, window,
    in_sem, x_send, x_recv, l_send, l_recv, s_send, s_recv,
    a_send, a_recv, b_send, b_recv, k_send, k_recv, g_send, g_recv, c_send, c_recv,
):
    def state(k):
        return types.SimpleNamespace(
            mu_v=mu_s.at[k], u0_v=u0_s.at[k], rs_v=rs_s.at[k], u=u_s.at[k], w=w_s.at[k],
            cx=cx_s.at[k], cy=cy_s.at[k], cz=cz_s.at[k], dint=dint_s.at[k], t0=t0_s.at[k],
            inv=inv_s.at[k], coef=coef_s.at[k], rhs=rhs_s.at[k], gx=gx_s.at[k], gy=gy_s.at[k],
            gz=gz_s.at[k], base=base_s.at[k], base_w=base_w_s.at[k], faces=faces_s.at[k],
            wfaces=wfaces_s.at[k], ghost=ghost_s.at[k], cface=cface_s.at[k], rel=rel_s.at[k],
            bnd=bnd_s.at[k], corr=corr_s.at[k],
        )

    own, rim = state(0), state(1)
    both = (own, rim)
    grp, sub = lax.axis_index("grp"), lax.axis_index("sub")
    devices = n_grp * n_sub
    me = grp * n_sub + sub

    def dev(by):
        other = lax.rem(me + by + devices, devices)
        return (lax.div(other, n_sub), lax.rem(other, n_sub))

    def in_group(by):
        return (grp, lax.rem(sub + by + n_sub, n_sub))

    def across(by):
        return (lax.rem(grp + by + n_grp, n_grp), sub)

    def has(by):
        return (me + by >= 0) & (me + by < devices)

    barrier = pltpu.get_barrier_semaphore()

    def greet(to):
        pl.semaphore_signal(barrier, inc=1, device_id=to, device_id_type=MESH)

    greeted = n_sub - 1 + n_grp - 1
    for by in (1, -1, 2, -2):
        pl.when(has(by))(functools.partial(greet, dev(by)))
        greeted = greeted + has(by).astype(I32)
    for by in range(1, n_sub):
        greet(in_group(by))
    for by in range(1, n_grp):
        greet(across(by))

    loads = [
        pltpu.make_async_copy(a, b, in_sem.at[i])
        for i, (a, b) in enumerate(
            ((mu, own.mu_v), (neigh, nb_v), (pot, own.u0_v), (rs, own.rs_v), (owner, own_v))
        )
    ]
    for copy in loads:
        copy.start()

    lane = lax.broadcasted_iota(I32, (BLK, LN), 1)
    xpos = lane & 15
    yrow = lane >> 4
    row = lax.broadcasted_iota(I32, (BLK, LN), 0)
    lane8 = lax.broadcasted_iota(I32, (8, LN), 1)
    row8 = lax.broadcasted_iota(I32, (8, LN), 0)
    x_first, x_last = xpos == 0, xpos == BE - 1
    x_face = x_first | x_last
    y_first, y_last = lane < BE, lane >= LN - BE
    even = (lane & 1) == 0
    zero = jnp.zeros((BLK, LN), F32)

    def turn(v, by):
        if isinstance(by, int):
            by = by % LN
            return v if by == 0 else pltpu.roll(v, by, 1)
        return pltpu.roll(v, by & (LN - 1), 1)

    def lower_y(v0, v1):
        a, b = turn(v0, BE), turn(v1, BE)
        return a, jnp.where(y_first, a, b)

    def upper_y(v0, v1):
        a, b = turn(v0, -BE), turn(v1, -BE)
        return jnp.where(y_last, b, a), b

    def remote(src, dst, a, b, to):
        return pltpu.make_async_remote_copy(
            src_ref=src, dst_ref=dst, send_sem=a, recv_sem=b, device_id=to, device_id_type=MESH
        )

    def faces_of(produce, faces_ref, plane):
        for zg in range(2):
            def body(i, carry, zg=zg):
                x0, x1, y2, y3 = carry
                v0, v1 = produce(zg, i)
                here = (xpos == 2 * i) | (xpos == ((2 * i + 15) & 15))
                x0 = jnp.where(here, turn(v0, 2 * i), x0)
                x1 = jnp.where(here, turn(v1, 2 * i), x1)
                line = yrow == i
                y2 = jnp.where(line, turn(v0, BE * i), y2)
                y3 = jnp.where(line, turn(v1, BE * i + BE), y3)
                return x0, x1, y2, y3

            x0, x1, y2, y3 = steps(8, body, (zero, zero, zero, zero))
            faces_ref[8 + 2 * zg] = x0
            faces_ref[9 + 2 * zg] = x1
            faces_ref[4 + zg] = y2
            faces_ref[6 + zg] = y3
        for h in range(2):
            faces_ref[h] = plane(0, h)
            faces_ref[2 + h] = plane(BE - 1, h)

    def sources(faces_ref, src_ref, is_rim=False):
        for k in range(12):
            if k < 8:
                v = faces_ref[SOURCE[k]]
            else:
                x = faces_ref[k]
                v = jnp.where(even, turn(x, -15), turn(x, 15))
            if is_rim:
                src_ref[k, 8:16, :] = v[0:8]
                src_ref[k, 32:40, :] = v[8:16]
            else:
                src_ref[k, 16:32, :] = v

    def send_faces(src_ref, slot):
        for m in range(6):
            pair = []
            for k in (2 * m, 2 * m + 1):
                edge = jnp.where(row8 < 4, src_ref[k, 16:24, :], src_ref[k, 24:32, :])
                way = route[GROUP[k]]
                d = jnp.zeros((8, LN), F32)
                for r in (4,) if k < 4 else range(1, 8):
                    d = jnp.where(way == r, pltpu.roll(edge, r, 0), d)
                pair.append(d)
                if slot:
                    keep[slot - 1, k] = d
            d0, d1 = pair
            send[slot, 0, m] = jnp.where(row8 < 4, d0, pltpu.roll(d1, 4, 0))
            send[slot, 1, m] = jnp.where(row8 < 4, pltpu.roll(d0, 4, 0), d1)
        start(face_copies(slot))

    def face_copies(slot):
        return [
            (
                remote(
                    send.at[slot, way],
                    recv.at[slot, way],
                    x_send.at[slot, way],
                    x_recv.at[slot, way],
                    dev(1 - 2 * way),
                ),
                1 - 2 * way,
            )
            for way in range(2)
        ]

    def local_ghosts(src_ref, ghost_ref):
        for k in range(12):
            r = rel_local[GROUP[k]]
            g = zero
            for by in (-4, 4) if k < 4 else range(-4, 5):
                g = jnp.where(r == by, src_ref[k, 16 + by : 32 + by, :], g)
            ghost_ref[k] = g

    def all_ghosts(src_ref, st):
        for k in range(12):
            r = st.rel[GROUP[k]]
            tops = (8, 32) if st is rim else (16, 24)
            for t in range(2):
                g = jnp.zeros((8, LN), F32)
                rt = r[8 * t : 8 * t + 8]
                for by in (-4, 4) if k < 4 else range(-4, 5):
                    g = jnp.where(rt == by, src_ref[k, tops[t] + by : tops[t] + by + 8, :], g)
                st.ghost[k, 8 * t : 8 * t + 8, :] = g

    def add_remote(slot, near_ref, ghost_ref):
        arrive(face_copies(slot))
        for m in range(6):
            lo, hi = recv[slot, 0, m], recv[slot, 1, m]
            lo1, hi0 = pltpu.roll(lo, 4, 0), pltpu.roll(hi, 4, 0)
            a, b = 2 * m, 2 * m + 1
            ghost_ref[a, 0:8, :] = near_ref[a, 0:8, :] + jnp.where(row8 < 4, lo, 0.0)
            ghost_ref[b, 0:8, :] = near_ref[b, 0:8, :] + jnp.where(row8 < 4, lo1, 0.0)
            ghost_ref[a, 8:16, :] = near_ref[a, 8:16, :] + jnp.where(row8 < 4, 0.0, hi0)
            ghost_ref[b, 8:16, :] = near_ref[b, 8:16, :] + jnp.where(row8 < 4, 0.0, hi)

    def rows_both_ways(src, dst, a, b):
        return [
            (remote(src(8), dst(0), a.at[0], b.at[0], dev(1)), 1),
            (remote(src(0), dst(8), a.at[1], b.at[1], dev(-1)), -1),
        ]

    def field_copies(k):
        ref = (mu_s, u0_s, rs_s)[k]
        return rows_both_ways(
            lambda r: ref.at[0, pl.ds(r, 8)],
            lambda r: ref.at[1, pl.ds(r, 8)],
            k_send.at[k],
            k_recv.at[k],
        )

    def ghost_copies(slot):
        return rows_both_ways(
            lambda r: near_local.at[slot, :, pl.ds(r, 8)],
            lambda r: near_far.at[slot, :, pl.ds(r, 8)],
            g_send.at[slot],
            g_recv.at[slot],
        )

    def coupling_copies():
        return rows_both_ways(
            lambda r: cface_s.at[0, :, pl.ds(r, 8)],
            lambda r: cface_s.at[1, :, pl.ds(r, 8)],
            c_send,
            c_recv,
        )

    def start(copies):
        for copy, by in copies:
            if by is None:
                copy.start()
            else:
                pl.when(has(by))(copy.start)

    def arrive(copies):
        for copy, by in copies:
            if by is None:
                copy.wait_recv()
            else:
                pl.when(has(-by))(copy.wait_recv)

    def finish(copies):
        for copy, by in copies:
            if by is None:
                copy.wait_send()
            else:
                pl.when(has(by))(copy.wait_send)

    def rim_ghosts(slot):
        arrive(ghost_copies(slot))
        for k in range(12):
            d = keep[slot, k]
            rim.ghost[k, 0:8, :] = near_far[slot, k, 0:8, :] + jnp.where(row8 < 4, 0.0, d)
            rim.ghost[k, 8:16, :] = near_far[slot, k, 8:16, :] + jnp.where(row8 < 4, d, 0.0)

    def spread_x(faces_ref, zg, i, h):
        return turn(faces_ref[8 + 2 * zg + h], LN - 2 * i)

    def spread_y(faces_ref, zg, i, h):
        return turn(faces_ref[(4, 6)[h] + zg], LN - BE * i - (0, BE)[h])

    first = BLK * me - MINE
    loads[1].wait()
    low = lax.div(first + LN, LN) - 1
    shift = first - low * LN
    tiles = nblk // LN

    def table(k):
        at = pl.multiple_of(lax.rem(k + tiles, tiles) * LN, LN)
        rows6 = nb_v[:, pl.ds(at, LN)]
        return jnp.concatenate([rows6, jnp.full((2, LN), -1, I32)], axis=0)

    back = LN - shift
    ta, tb = turn(table(low), back), turn(table(low + 1), back)
    ids = first + lane8
    nb = jnp.where(lane8 < back, ta, tb)
    nb = jnp.where((nb >= 0) & (ids >= 0) & (ids < nblk), nb - first, -1000).astype(F32)
    nbt = nb.T
    col[...] = nbt

    def columns(f, lo, n):
        return jnp.broadcast_to(col[lo : lo + n, f : f + 1], (n, LN))

    rowf = row.astype(F32)
    row8f = row8.astype(F32)
    rim_row = jnp.where(row < 8, rowf + (MINE - 8.0), rowf + (MINE + 8.0))
    far = jnp.zeros((BLK, LN), F32) + 99.0
    rels, routes, edges, full, rim_full, rim_edges = [], [], [], [], [], []
    for f in range(6):
        to = columns(f, MINE, 16)
        step = to - float(MINE) - rowf
        near = (to >= float(MINE)) & (to < MINE + 16.0)
        rels.append(jnp.where(near, step, far))
        full.append(step)
        edges.append(jnp.where(to < 0.0, 1.0, 0.0))
        before, after = columns(f, MINE - 8, 8), columns(f, MINE + 16, 8)
        to = jnp.concatenate([before, after], axis=0)
        rim_full.append(to - rim_row)
        rim_edges.append(jnp.where(to < 0.0, 1.0, 0.0))
        to8 = jnp.where(row8 < 4, after, before)
        j = jnp.where(row8 < 4, to8 - (MINE + 8.0), to8 - float(MINE))
        ok = jnp.where(row8 < 4, jnp.where(j >= 4.0, 1.0, 0.0), jnp.where(j >= 0.0, 1.0, 0.0))
        ok = ok * jnp.where(row8 < 4, jnp.where(j < 8.0, 1.0, 0.0), jnp.where(j < 4.0, 1.0, 0.0))
        r = row8f - j
        routes.append(jnp.where(ok > 0.5, jnp.where(r < 0.0, r + 8.0, r), 99.0))
    even8 = (lane8 & 1) == 0
    for g in range(4):
        rel_local[g], route[g] = rels[g], routes[g]
        own.rel[g], own.bnd[g] = full[g], edges[g]
        rim.rel[g], rim.bnd[g] = rim_full[g], rim_edges[g]
    rel_local[4] = jnp.where(even, rels[4], rels[5])
    route[4] = jnp.where(even8, routes[4], routes[5])
    own.rel[4] = jnp.where(even, full[4], full[5])
    own.bnd[4] = jnp.where(even, edges[4], edges[5])
    rim.rel[4] = jnp.where(even, rim_full[4], rim_full[5])
    rim.bnd[4] = jnp.where(even, rim_edges[4], rim_edges[5])
    for st, e in ((own, edges), (rim, rim_edges)):
        st.bx = jnp.where(x_first, e[4], jnp.where(x_last, e[5], 0.0))
        st.by = (jnp.where(y_first, e[2], 0.0), jnp.where(y_last, e[3], 0.0))

    def fill_way(way):
        for slot in range(N_X):
            for m in range(6):
                recv[slot, way, m] = jnp.zeros((8, LN), F32)

    def fill_blocks(by):
        at = MINE + 16 * by
        link_w[at : at + 16] = jnp.ones((16, LN), F32)
        share_w[at : at + 16] = jnp.zeros((16, LN), F32)

    for way in range(2):
        pl.when(jnp.logical_not(has(2 * way - 1)))(functools.partial(fill_way, way))
    for by in (1, -1, 2, -2):
        pl.when(jnp.logical_not(has(by)))(functools.partial(fill_blocks, by))

    def plane_of(ref):
        return lambda z, h: ref[:, z * 256 + h * LN : z * 256 + (h + 1) * LN]

    def from_input(ref, store=None):
        def produce(zg, i):
            at = pl.multiple_of((zg * 8 + i) * 256, 256)
            v0, v1 = ref[:, pl.ds(at, LN)], ref[:, pl.ds(at + LN, LN)]
            if store is not None:
                store[zg * 8 + i + 1, :, chunk(0)] = v0
                store[zg * 8 + i + 1, :, chunk(1)] = v1
            return v0, v1

        return produce

    loads[0].wait()
    faces_of(from_input(own.mu_v), own_mu, plane_of(own.mu_v))
    sources(own_mu, src_w)
    pl.semaphore_wait(barrier, greeted)
    send_faces(src_w, X_MU)
    loads[2].wait()
    faces_of(from_input(own.u0_v, own.u), own.faces, plane_of(own.u0_v))
    sources(own.faces, src_f)
    send_faces(src_f, X_U0)
    local_ghosts(src_f, near_local.at[0])
    start(ghost_copies(0))
    loads[3].wait()
    start(field_copies(0))
    start(field_copies(2))

    local_ghosts(src_w, mu_f)
    for st in both:
        for ref in (st.u, st.w):
            ref[0] = jnp.zeros((BLK, 256), F32)
            ref[BE + 1] = jnp.zeros((BLK, 256), F32)
        st.cz[0] = jnp.zeros((BLK, 256), F32)
        st.cz[BE] = jnp.zeros((BLK, 256), F32)

    def mean(a, b):
        return 2.0 * a * b / (a + b)

    def inner_couplings(st):
        def body(z):
            at = pl.multiple_of(z * 256, 256)
            m0, m1 = st.mu_v[:, pl.ds(at, LN)], st.mu_v[:, pl.ds(at + LN, LN)]
            y0, y1 = lower_y(m0, m1)
            st.cx[z, :, chunk(0)] = jnp.where(x_first, 0.0, mean(m0, turn(m0, 1)))
            st.cx[z, :, chunk(1)] = jnp.where(x_first, 0.0, mean(m1, turn(m1, 1)))
            st.cy[z, :, chunk(0)] = jnp.where(y_first, 0.0, mean(m0, y0))
            st.cy[z, :, chunk(1)] = mean(m1, y1)

        def across_z(z):
            at = pl.multiple_of(z * 256, 256)
            st.cz[z + 1] = mean(st.mu_v[:, pl.ds(at, 256)], st.mu_v[:, pl.ds(at + 256, 256)])

        steps(BE, body)
        steps(BE - 1, across_z)

    inner_couplings(own)

    def around(st, z):
        cx0, cx1 = st.cx[z, :, chunk(0)], st.cx[z, :, chunk(1)]
        cy0, cy1 = st.cy[z, :, chunk(0)], st.cy[z, :, chunk(1)]
        uy0, uy1 = upper_y(cy0, cy1)
        uy1 = jnp.where(y_last, 0.0, uy1)
        lo = (st.cz[z, :, chunk(0)], st.cz[z, :, chunk(1)])
        up = (st.cz[z + 1, :, chunk(0)], st.cz[z + 1, :, chunk(1)])
        return (
            (lo[0], up[0], cy0, uy0, cx0, turn(cx0, -1)),
            (lo[1], up[1], cy1, uy1, cx1, turn(cx1, -1)),
        )

    def beside(ref, z):
        v0, v1 = ref[z + 1, :, chunk(0)], ref[z + 1, :, chunk(1)]
        l0, l1 = lower_y(v0, v1)
        p0, p1 = upper_y(v0, v1)
        return (v0, v1), (
            (ref[z, :, chunk(0)], ref[z + 2, :, chunk(0)], l0, p0, turn(v0, 1), turn(v0, -1)),
            (ref[z, :, chunk(1)], ref[z + 2, :, chunk(1)], l1, p1, turn(v1, 1), turn(v1, -1)),
        )

    def first_terms(st):
        def body(z, acc):
            c = around(st, z)
            _, n = beside(st.u, z)
            for h in range(2):
                at = pl.multiple_of(z * 256 + h * LN, LN)
                r = st.rs_v[:, pl.ds(at, LN)]
                d = c[h][0]
                t = r + c[h][0] * n[h][0]
                for f in range(1, 6):
                    d = d + c[h][f]
                    t = t + c[h][f] * n[h][f]
                st.dint[z, :, chunk(h)] = d
                st.t0[z, :, chunk(h)] = t
                acc = acc + r
            return acc

        return steps(BE, body, zero)

    acc = first_terms(own)
    rsum[...] = jnp.broadcast_to(jnp.sum(acc, axis=1, keepdims=True), (BLK, LN))

    add_remote(X_MU, mu_f, own.ghost)
    for k in range(12):
        m = own_mu[k]
        g = jnp.where(own.bnd[GROUP[k]] > 0.5, m, own.ghost[k])
        own.cface[k] = mean(m, g)
    add_remote(X_U0, near_local.at[0], own.ghost)

    def add_first_z(st):
        for k in range(12):
            pface[k] = st.cface[k] * st.ghost[k]
        for h in range(2):
            st.dint[0, :, chunk(h)] += st.cface[h]
            st.dint[BE - 1, :, chunk(h)] += st.cface[2 + h]
            st.t0[0, :, chunk(h)] += pface[h]
            st.t0[BE - 1, :, chunk(h)] += pface[2 + h]

    y_face = (y_first, y_last)

    def sweep_first(st):
        def produce(zg, i):
            z = zg * 8 + i
            vs = []
            for h in range(2):
                d = st.dint[z, :, chunk(h)]
                t = st.t0[z, :, chunk(h)]
                d = d + jnp.where(x_face, spread_x(st.cface, zg, i, h), 0.0)
                d = d + jnp.where(y_face[h], spread_y(st.cface, zg, i, h), 0.0)
                t = t + jnp.where(x_face, spread_x(pface, zg, i, h), 0.0)
                t = t + jnp.where(y_face[h], spread_y(pface, zg, i, h), 0.0)
                q = RELAX_FINE / d
                st.inv[z, :, chunk(h)] = q
                v = (1.0 - RELAX_FINE) * st.u[z + 1, :, chunk(h)] + q * t
                st.u[z + 1, :, chunk(h)] = v
                vs.append(v)
            return vs

        return produce

    def each_plane(produce):
        for zg in range(2):
            steps(8, lambda i, zg=zg: (produce(zg, i), None)[1])

    def plane_u(ref):
        return lambda z, h: ref[z + 1, :, chunk(h)]

    add_first_z(own)
    faces_of(sweep_first(own), own.faces, plane_u(own.u))
    sources(own.faces, src_f)
    send_faces(src_f, X_U1)
    start(field_copies(1))

    def coefficients(st):
        for h in range(2):
            st.gz[0, :, chunk(h)] = st.cface[h] * st.inv[0, :, chunk(h)]
            st.gz[1, :, chunk(h)] = st.cface[2 + h] * st.inv[BE - 1, :, chunk(h)]

        def produce(zg, i):
            z = zg * 8 + i
            c = around(st, z)
            for h in range(2):
                q = st.inv[z, :, chunk(h)]
                for f in range(6):
                    st.coef[f, z, :, chunk(h)] = c[h][f] * q
                at = pl.multiple_of(z * 256 + h * LN, LN)
                st.rhs[z, :, chunk(h)] = st.rs_v[:, pl.ds(at, LN)] * q
                fx = jnp.where(x_face, spread_x(st.cface, zg, i, h), 0.0) * q
                fy = jnp.where(y_face[h], spread_y(st.cface, zg, i, h), 0.0) * q
                st.gx[z, :, chunk(h)] = fx
                st.gy[z, :, chunk(h)] = fy
                st.w[z + 1, :, chunk(h)] = 1.0 - fx * st.bx - fy * st.by[h]

        each_plane(produce)
        for h in range(2):
            st.w[1, :, chunk(h)] -= st.gz[0, :, chunk(h)] * st.bnd[0]
            st.w[BE, :, chunk(h)] -= st.gz[1, :, chunk(h)] * st.bnd[1]

    def inner_sweep(st, ref, base_ref, with_rhs):
        def body(z):
            v, n = beside(ref, z)
            for h in range(2):
                b = (1.0 - RELAX_FINE) * v[h]
                if with_rhs:
                    b = b + st.rhs[z, :, chunk(h)]
                for f in range(6):
                    b = b + st.coef[f, z, :, chunk(h)] * n[h][f]
                base_ref[z, :, chunk(h)] = b

        steps(BE, body)

    def add_z(st, base_ref):
        for h in range(2):
            base_ref[0, :, chunk(h)] += st.gz[0, :, chunk(h)] * st.ghost[h]
            base_ref[BE - 1, :, chunk(h)] += st.gz[1, :, chunk(h)] * st.ghost[2 + h]

    def outer_sweep(st, base_ref, ref, fix=None):
        add_z(st, base_ref)

        def produce(zg, i):
            z = zg * 8 + i
            vs = []
            for h in range(2):
                v = base_ref[z, :, chunk(h)]
                if fix is not None:
                    v = v + fix
                v = v + st.gx[z, :, chunk(h)] * spread_x(st.ghost, zg, i, h)
                v = v + st.gy[z, :, chunk(h)] * spread_y(st.ghost, zg, i, h)
                ref[z + 1, :, chunk(h)] = v
                vs.append(v)
            return vs

        return produce

    local_ghosts(src_f, near_local.at[1])
    coefficients(own)
    inner_sweep(own, own.u, own.base, True)
    start(ghost_copies(1))
    start(coupling_copies())

    def face_sums(value):
        sums = []
        for f in range(4):
            s = value(2 * f) + value(2 * f + 1)
            sums.append(jnp.sum(s, axis=1, keepdims=True))
        s = value(8) + value(9) + value(10) + value(11)
        sums.append(jnp.sum(jnp.where(even, s, 0.0), axis=1, keepdims=True))
        sums.append(jnp.sum(jnp.where(even, 0.0, s), axis=1, keepdims=True))
        return sums

    links = face_sums(lambda k: own.cface[k])
    tile = zero
    link_total = links[0]
    for f in range(6):
        tile = jnp.where(lane == f, links[f], tile)
        if f:
            link_total = link_total + links[f]
    link_w[MINE : MINE + 16] = tile

    def spread_blocks(ref, a, b):
        mine = ref.at[pl.ds(MINE, 16)]
        return [
            (remote(mine, ref.at[pl.ds(MINE - 16 * by, 16)], a.at[i], b.at[i], dev(by)), by)
            for i, by in enumerate((1, -1, 2, -2))
        ]

    link_copies = spread_blocks(link_w, l_send, l_recv)
    start(link_copies)


    add_remote(X_U1, near_local.at[1], own.ghost)
    faces_of(outer_sweep(own, own.base, own.u), own.faces, plane_u(own.u))
    sources(own.faces, src_f)
    send_faces(src_f, X_U2)
    local_ghosts(src_f, near_local.at[2])
    start(ghost_copies(2))

    sums = face_sums(lambda k: own.cface[k] * own.faces[k])
    left = rsum[:, 0:1]
    group_left = left
    tile = zero
    for f in range(6):
        tile = jnp.where(lane == f, sums[f], tile)
        left = left - sums[f]
        group_left = group_left - sums[f] * edges[f][:, 0:1]
    share_w[MINE : MINE + 16] = jnp.where(lane == 6, left, tile)
    share_copies = spread_blocks(share_w, s_send, s_recv)
    start(share_copies)
    total[0] = jnp.where(
        lane8 < 64,
        jnp.sum(group_left, axis=0, keepdims=True),
        jnp.sum(link_total, axis=0, keepdims=True),
    )
    total_copies = [
        (remote(total.at[0], total.at[i], a_send.at[i], a_recv.at[i], in_group(i)), None)
        for i in range(1, n_sub)
    ]
    start(total_copies)

    inner_sweep(own, own.u, own.base, True)
    arrive(field_copies(0))
    inner_couplings(rim)
    arrive(field_copies(1) + field_copies(2))
    each_plane(from_input(rim.u0_v, rim.u))
    first_terms(rim)
    arrive(coupling_copies())
    rim_ghosts(0)
    add_first_z(rim)
    each_plane(sweep_first(rim))
    coefficients(rim)
    inner_sweep(rim, rim.u, rim.base, True)
    rim_ghosts(1)
    each_plane(outer_sweep(rim, rim.base, rim.u))
    inner_sweep(rim, rim.u, rim.base, True)

    arrive(link_copies)
    iw = lax.broadcasted_iota(I32, (WIN, WIN), 0)
    lw = lax.broadcasted_iota(I32, (WIN, WIN), 1)
    lwf = lw.astype(F32)
    diagonal = link_w[:, 0:1]
    for f in range(1, 6):
        diagonal = diagonal + link_w[:, f : f + 1]
    gain = RELAX_COARSE / diagonal
    ident = jnp.where(iw == lw, 1.0, 0.0)
    hot = [jnp.where(col[0:WIN, f : f + 1] == lwf, 1.0, 0.0) for f in range(6)]
    gmat = link_w[:, 0:1] * hot[0]
    for f in range(1, 6):
        gmat = gmat + link_w[:, f : f + 1] * hot[f]
    gmat = gmat * gain + (1.0 - RELAX_COARSE) * ident

    def product(a, b):
        return lax.dot_general(
            a,
            b,
            (((1,), (0,)), ((), ())),
            precision=lax.Precision.HIGHEST,
            preferred_element_type=F32,
        )

    ymat = ident + gmat
    ymat = ident + product(ymat, gmat)
    ymat = ident + product(ymat, gmat)
    scale = jnp.sum(ident * gain, axis=0, keepdims=True)

    def pick(m):
        return [m[MINE : MINE + 16], m[MINE - 8 : MINE], m[MINE + 16 : MINE + 24]]

    picks = jnp.concatenate(sum([pick(m) for m in [ident] + hot], []), axis=0)
    qmat[...] = product(picks, ymat) * scale

    arrive(total_copies)
    part = total[0]
    for i in range(1, n_sub):
        part = part + total[i]
    group_total[0] = part
    group_copies = [
        (remote(group_total.at[0], group_total.at[i], b_send.at[i], b_recv.at[i], across(i)), None)
        for i in range(1, n_grp)
    ]
    start(group_copies)

    def from_w(st):
        def produce(zg, i):
            z = zg * 8 + i
            return st.w[z + 1, :, chunk(0)], st.w[z + 1, :, chunk(1)]

        return produce

    for st in both:
        faces_of(from_w(st), st.wfaces, plane_u(st.w))
        sources(st.wfaces, src_w, st is rim)
        inner_sweep(st, st.w, st.base_w, False)
    for st in both:
        all_ghosts(src_w, st)
        each_plane(outer_sweep(st, st.base_w, st.w))

    arrive(share_copies)
    acc = ident * share_w[:, 6:7]
    iwf = iw.astype(F32)
    for f in range(6):
        acc = acc + jnp.where(nb[f : f + 1, 0:WIN] == iwf, share_w[:, (f ^ 1) : (f ^ 1) + 1], 0.0)
    source_row = jnp.sum(acc, axis=0, keepdims=True)
    fixed = jnp.sum(qmat[...] * source_row, axis=1, keepdims=True)
    for n, st in enumerate(both):
        fix = fixed[16 * n : 16 * n + 16]
        st.corr[0] = jnp.broadcast_to(fix, (BLK, LN))
        gains = []
        for f in range(6):
            at = 32 * (f + 1) + 16 * n
            gains.append(jnp.broadcast_to(fixed[at : at + 16] - fix, (BLK, LN)))
        for f in range(4):
            st.corr[1 + f] = gains[f]
        st.corr[5] = jnp.where(even, gains[4], gains[5])

    def third_sweep(st):
        for k in range(12):
            st.ghost[k] += st.corr[1 + GROUP[k]]
        produce = outer_sweep(st, st.base, st.u, st.corr[0])
        faces_of(produce, st.faces, plane_u(st.u))
        sources(st.faces, src_f, st is rim)

    add_remote(X_U2, near_local.at[2], own.ghost)
    third_sweep(own)
    inner_sweep(own, own.u, own.base, True)
    rim_ghosts(2)
    third_sweep(rim)
    inner_sweep(rim, rim.u, rim.base, True)
    for st in both:
        all_ghosts(src_f, st)

    arrive(group_copies)
    part = group_total[0]
    for i in range(1, n_grp):
        part = part + group_total[i]
    level = part[0:1, 0:1] / part[0:1, 64:65]
    level = jnp.broadcast_to(level, (BLK, LN))

    def last_sweep(st):
        add_z(st, st.base)

        def produce(zg, i):
            z = zg * 8 + i
            for h in range(2):
                v = st.base[z, :, chunk(h)] + level * st.w[z + 1, :, chunk(h)]
                v = v + st.gx[z, :, chunk(h)] * spread_x(st.ghost, zg, i, h)
                v = v + st.gy[z, :, chunk(h)] * spread_y(st.ghost, zg, i, h)
                if st is rim:
                    window[2 * z + h, 0:8, :] = v[0:8]
                    window[2 * z + h, 24:32, :] = v[8:16]
                else:
                    window[2 * z + h, 8:24, :] = v

        each_plane(produce)

    for st in both:
        last_sweep(st)

    loads[4].wait()
    owners = own_v[...]
    starts = jnp.sum(jnp.where(owners < me, 1.0, 0.0)).astype(I32)
    count = jnp.sum(jnp.where(owners == me, 1.0, 0.0)).astype(I32)
    at = jnp.clip(starts - BLK * me + 8, 4, 12)
    row24 = lax.broadcasted_iota(I32, (CAP, LN), 0)
    live = row24 < count

    def emit(z):
        for h in range(2):
            lanes = pl.ds(pl.multiple_of(z * 256 + h * LN, LN), LN)
            out[:, lanes] = jnp.where(live, window[2 * z + h, pl.ds(at, CAP), :], 0.0)

    steps(BE, emit)

    for slot in range(N_X):
        finish(face_copies(slot))
    for slot in range(3):
        finish(ghost_copies(slot) + field_copies(slot))
    finish(coupling_copies() + link_copies + share_copies + total_copies + group_copies)


def local(potential, right_side, permeability, new_owner, neighbours):
    n_grp, n_sub = lax.axis_size("grp"), lax.axis_size("sub")
    nblk = new_owner.shape[0]
    vmem = pltpu.VMEM
    plane = (BLK, 256)
    dma = pltpu.SemaphoreType.DMA
    faces = (12, BLK, LN)
    scratch = [
        vmem((2, BLK, 4096), F32),
        vmem((2, BLK, 4096), F32),
        vmem((2, BLK, 4096), F32),
        vmem((nblk // LN, LN), I32),
        vmem((6, nblk), I32),
        vmem((2, BE + 2, *plane), F32),
        vmem((2, BE + 2, *plane), F32),
        vmem((2, BE, *plane), F32),
        vmem((2, BE, *plane), F32),
        vmem((2, BE + 1, *plane), F32),
        vmem((2, BE, *plane), F32),
        vmem((2, BE, *plane), F32),
        vmem((2, BE, *plane), F32),
        vmem((2, 6, BE, *plane), F32),
        vmem((2, BE, *plane), F32),
        vmem((2, BE, *plane), F32),
        vmem((2, BE, *plane), F32),
        vmem((2, 2, *plane), F32),
        vmem((2, BE, *plane), F32),
        vmem((2, BE, *plane), F32),
        vmem((2, *faces), F32),
        vmem((2, *faces), F32),
        vmem((2, *faces), F32),
        vmem((2, *faces), F32),
        vmem((2, 5, BLK, LN), F32),
        vmem((2, 5, BLK, LN), F32),
        vmem((2, 6, BLK, LN), F32),
        vmem(faces, F32),
        vmem(faces, F32),
        vmem(faces, F32),
        vmem((12, 48, LN), F32),
        vmem((12, 48, LN), F32),
        vmem((3, *faces), F32),
        vmem((3, *faces), F32),
        vmem((3, 12, 8, LN), F32),
        vmem((5, BLK, LN), F32),
        vmem((5, 8, LN), F32),
        vmem((LN, 8), F32),
        vmem((224, WIN), F32),
        vmem((WIN, LN), F32),
        vmem((WIN, LN), F32),
        vmem((BLK, LN), F32),
        vmem((N_X, 2, 6, 8, LN), F32),
        vmem((N_X, 2, 6, 8, LN), F32),
        vmem((n_sub, 8, LN), F32),
        vmem((n_grp, 8, LN), F32),
        vmem((32, 40, LN), F32),
        dma((5,)),
        dma((N_X, 2)),
        dma((N_X, 2)),
        dma((4,)),
        dma((4,)),
        dma((4,)),
        dma((4,)),
        dma((n_sub,)),
        dma((n_sub,)),
        dma((n_grp,)),
        dma((n_grp,)),
        dma((3, 2)),
        dma((3, 2)),
        dma((3, 2)),
        dma((3, 2)),
        dma((2,)),
        dma((2,)),
    ]
    return pl.pallas_call(
        functools.partial(kernel, n_grp, n_sub, nblk),
        out_shape=jax.ShapeDtypeStruct((CAP, 4096), F32),
        in_specs=[pl.BlockSpec(memory_space=pl.ANY)] * 5,
        out_specs=pl.BlockSpec(memory_space=pltpu.VMEM),
        scratch_shapes=scratch,
        compiler_params=pltpu.CompilerParams(
            collective_id=0, has_side_effects=True, vmem_limit_bytes=60 * 1024 * 1024
        ),
        cost_estimate=pl.CostEstimate(
            flops=8_000_000, bytes_accessed=1_200_000, transcendentals=0
        ),
        name="cycle",
    )(potential, right_side, permeability, new_owner.reshape(nblk // LN, LN), neighbours)


def solution(mesh):
    in_specs = (P(("grp", "sub"), None), P(("grp", "sub"), None), P(("grp", "sub"), None), P(), P())
    out_specs = P(("grp", "sub"), None)
    return jax.shard_map(local, mesh=mesh, in_specs=in_specs, out_specs=out_specs, check_vma=False)
```

time: 43.7 us -> 36 us (0.82)
  Pallas kernels: 38.3 us -> 34.1 us
  local copies, waits for them, and re-layouts: 5.13 us -> 1.77 us
    pallas_call x1, Pallas kernels: 38.3 us -> 34.1 us  [local(): pl.pallas_call(functools.partial(kernel, n_grp, n_sub, nblk), out_shape=j...]
    unnamed x11 -> x1, local copies, waits for them, and re-layouts: 5.13 us -> 1.77 us
where the time goes in v2:
time: 36 us; the launch traced here: 35.8 us
  Pallas kernels  34.1 us (95%)
  local copies, waits for them, and re-layouts  1.77 us (5%)
    pallas_call x1, Pallas kernels, local(): pl.pallas_call(functools.partial(kernel, n_grp, n_sub, nblk), out_shape=j...  34.1 us
    unnamed x1, local copies, waits for them, and re-layouts  1.77 us

profile of v2, /device:TPU:1, one launch (start us, length us, event | category | flops | bytes accessed | tf_op | source)
XLA Modules:
  0.0 35.8 jit_solution(10411342257464585552)
XLA Ops:
  0.0 34.1 %cycle.1 = f32[24,4096]{1,0:T(8,128)} custom-call(f32[16,4096]{1,0:T(8,128)} %pot.1, f32[16,4096]{1,0:T(8,128)} %rs.1, f32[16,4096]{1,0:T(8,128)} %mu.1, s32[16,128]{1,0:T(8,128)} %bitcast.1, s32[6,2048]{1,0:T(8,128)} %neigh.1), custom_call_target="tpu_custom_call" | custom-call | flops 8000000 | bytes 1200000 | tf_op jit(solution)/shard_map/cycle/pallas_call | solution.py:882
  34.1 1.8 %copy.7 = f32[24,4096]{1,0:T(8,128)} copy(f32[24,4096]{1,0:T(8,128)} %cycle.1) | data formatting | bytes 786432

commit v3 on v2

--- a/solution.py
+++ b/solution.py
@@ -235,10 +235,11 @@
         ]
 
     def field_copies(k):
-        ref = (mu_s, u0_s, rs_s)[k]
+        ref = (mu_s, u0_s, rs_s, u0_s)[k]
+        lanes = {1: pl.ds(0, 2048), 3: pl.ds(2048, 2048)}.get(k, pl.ds(0, 4096))
         return rows_both_ways(
-            lambda r: ref.at[0, pl.ds(r, 8)],
-            lambda r: ref.at[1, pl.ds(r, 8)],
+            lambda r: ref.at[0, pl.ds(r, 8), lanes],
+            lambda r: ref.at[1, pl.ds(r, 8), lanes],
             k_send.at[k],
             k_recv.at[k],
         )
@@ -391,10 +392,10 @@
     sources(own.faces, src_f)
     send_faces(src_f, X_U0)
     local_ghosts(src_f, near_local.at[0])
-    start(ghost_copies(0))
     loads[3].wait()
     start(field_copies(0))
     start(field_copies(2))
+    start(field_copies(3))
 
     local_ghosts(src_w, mu_f)
     for st in both:
@@ -519,6 +520,7 @@
     sources(own.faces, src_f)
     send_faces(src_f, X_U1)
     start(field_copies(1))
+    start(ghost_copies(0))
 
     def coefficients(st):
         for h in range(2):
@@ -619,11 +621,6 @@
 
     add_remote(X_U1, near_local.at[1], own.ghost)
     faces_of(outer_sweep(own, own.base, own.u), own.faces, plane_u(own.u))
-    sources(own.faces, src_f)
-    send_faces(src_f, X_U2)
-    local_ghosts(src_f, near_local.at[2])
-    start(ghost_copies(2))
-
     sums = face_sums(lambda k: own.cface[k] * own.faces[k])
     left = rsum[:, 0:1]
     group_left = left
@@ -633,8 +630,6 @@
         left = left - sums[f]
         group_left = group_left - sums[f] * edges[f][:, 0:1]
     share_w[MINE : MINE + 16] = jnp.where(lane == 6, left, tile)
-    share_copies = spread_blocks(share_w, s_send, s_recv)
-    start(share_copies)
     total[0] = jnp.where(
         lane8 < 64,
         jnp.sum(group_left, axis=0, keepdims=True),
@@ -646,10 +641,17 @@
     ]
     start(total_copies)
 
+    sources(own.faces, src_f)
+    send_faces(src_f, X_U2)
+    share_copies = spread_blocks(share_w, s_send, s_recv)
+    start(share_copies)
+    local_ghosts(src_f, near_local.at[2])
+    start(ghost_copies(2))
+
     inner_sweep(own, own.u, own.base, True)
     arrive(field_copies(0))
     inner_couplings(rim)
-    arrive(field_copies(1) + field_copies(2))
+    arrive(field_copies(1) + field_copies(2) + field_copies(3))
     each_plane(from_input(rim.u0_v, rim.u))
     first_terms(rim)
     arrive(coupling_copies())
@@ -661,6 +663,17 @@
     rim_ghosts(1)
     each_plane(outer_sweep(rim, rim.base, rim.u))
     inner_sweep(rim, rim.u, rim.base, True)
+
+    arrive(total_copies)
+    part = total[0]
+    for i in range(1, n_sub):
+        part = part + total[i]
+    group_total[0] = part
+    group_copies = [
+        (remote(group_total.at[0], group_total.at[i], b_send.at[i], b_recv.at[i], across(i)), None)
+        for i in range(1, n_grp)
+    ]
+    start(group_copies)
 
     arrive(link_copies)
     iw = lax.broadcasted_iota(I32, (WIN, WIN), 0)
@@ -696,17 +709,6 @@
 
     picks = jnp.concatenate(sum([pick(m) for m in [ident] + hot], []), axis=0)
     qmat[...] = product(picks, ymat) * scale
-
-    arrive(total_copies)
-    part = total[0]
-    for i in range(1, n_sub):
-        part = part + total[i]
-    group_total[0] = part
-    group_copies = [
-        (remote(group_total.at[0], group_total.at[i], b_send.at[i], b_recv.at[i], across(i)), None)
-        for i in range(1, n_grp)
-    ]
-    start(group_copies)
 
     def from_w(st):
         def produce(zg, i):
@@ -803,6 +805,7 @@
         finish(face_copies(slot))
     for slot in range(3):
         finish(ghost_copies(slot) + field_copies(slot))
+    finish(field_copies(3))
     finish(coupling_copies() + link_copies + share_copies + total_copies + group_copies)
 
 
@@ -872,8 +875,8 @@
         dma((n_sub,)),
         dma((n_grp,)),
         dma((n_grp,)),
-        dma((3, 2)),
-        dma((3, 2)),
+        dma((4, 2)),
+        dma((4, 2)),
         dma((3, 2)),
         dma((3, 2)),
         dma((2,)),

time: 36 us -> 35.2 us (0.978)
  Pallas kernels: 34.1 us -> 33.2 us
    pallas_call x1, Pallas kernels: 34.1 us -> 33.2 us  [local(): pl.pallas_call(functools.partial(kernel, n_grp, n_sub, nblk), out_shape=j...]
where the time goes in v3:
time: 35.2 us; the launch traced here: 35 us
  Pallas kernels  33.2 us (94%)
  local copies, waits for them, and re-layouts  1.77 us (5%)
    pallas_call x1, Pallas kernels, local(): pl.pallas_call(functools.partial(kernel, n_grp, n_sub, nblk), out_shape=j...  33.2 us
    unnamed x1, local copies, waits for them, and re-layouts  1.77 us

profile of v3, /device:TPU:1, one launch (start us, length us, event | category | flops | bytes accessed | tf_op | source)
XLA Modules:
  0.0 35.0 jit_solution(3138759458752111468)
XLA Ops:
  0.0 33.2 %cycle.1 = f32[24,4096]{1,0:T(8,128)} custom-call(f32[16,4096]{1,0:T(8,128)} %pot.1, f32[16,4096]{1,0:T(8,128)} %rs.1, f32[16,4096]{1,0:T(8,128)} %mu.1, s32[16,128]{1,0:T(8,128)} %bitcast.1, s32[6,2048]{1,0:T(8,128)} %neigh.1), custom_call_target="tpu_custom_call" | custom-call | flops 8000000 | bytes 1200000 | tf_op jit(solution)/shard_map/cycle/pallas_call | solution.py:885
  33.2 1.8 %copy.7 = f32[24,4096]{1,0:T(8,128)} copy(f32[24,4096]{1,0:T(8,128)} %cycle.1) | data formatting | bytes 786432

commit v4 on v3

--- a/solution.py
+++ b/solution.py
@@ -44,8 +44,8 @@
     faces_s, wfaces_s, ghost_s, cface_s, rel_s, bnd_s, corr_s,
     pface, mu_f, own_mu, src_f, src_w, near_local, near_far, keep,
     rel_local, route, col, qmat, link_w, share_w, rsum,
-    send, recv, total, group_total, window,
-    in_sem, x_send, x_recv, l_send, l_recv, s_send, s_recv,
+    send, recv, total, group_total, window, window_w, out_v,
+    in_sem, o_sem, x_send, x_recv, l_send, l_recv, s_send, s_recv,
     a_send, a_recv, b_send, b_recv, k_send, k_recv, g_send, g_recv, c_send, c_recv,
 ):
     def state(k):
@@ -710,6 +710,23 @@
     picks = jnp.concatenate(sum([pick(m) for m in [ident] + hot], []), axis=0)
     qmat[...] = product(picks, ymat) * scale
 
+    def window_sweep(st, base_ref, win):
+        add_z(st, base_ref)
+
+        def produce(zg, i):
+            z = zg * 8 + i
+            for h in range(2):
+                v = base_ref[z, :, chunk(h)]
+                v = v + st.gx[z, :, chunk(h)] * spread_x(st.ghost, zg, i, h)
+                v = v + st.gy[z, :, chunk(h)] * spread_y(st.ghost, zg, i, h)
+                if st is rim:
+                    win[2 * z + h, 0:8, :] = v[0:8]
+                    win[2 * z + h, 24:32, :] = v[8:16]
+                else:
+                    win[2 * z + h, 8:24, :] = v
+
+        each_plane(produce)
+
     def from_w(st):
         def produce(zg, i):
             z = zg * 8 + i
@@ -723,7 +740,7 @@
         inner_sweep(st, st.w, st.base_w, False)
     for st in both:
         all_ghosts(src_w, st)
-        each_plane(outer_sweep(st, st.base_w, st.w))
+        window_sweep(st, st.base_w, window_w)
 
     arrive(share_copies)
     acc = ident * share_w[:, 6:7]
@@ -759,32 +776,8 @@
     for st in both:
         all_ghosts(src_f, st)
 
-    arrive(group_copies)
-    part = group_total[0]
-    for i in range(1, n_grp):
-        part = part + group_total[i]
-    level = part[0:1, 0:1] / part[0:1, 64:65]
-    level = jnp.broadcast_to(level, (BLK, LN))
-
-    def last_sweep(st):
-        add_z(st, st.base)
-
-        def produce(zg, i):
-            z = zg * 8 + i
-            for h in range(2):
-                v = st.base[z, :, chunk(h)] + level * st.w[z + 1, :, chunk(h)]
-                v = v + st.gx[z, :, chunk(h)] * spread_x(st.ghost, zg, i, h)
-                v = v + st.gy[z, :, chunk(h)] * spread_y(st.ghost, zg, i, h)
-                if st is rim:
-                    window[2 * z + h, 0:8, :] = v[0:8]
-                    window[2 * z + h, 24:32, :] = v[8:16]
-                else:
-                    window[2 * z + h, 8:24, :] = v
-
-        each_plane(produce)
-
     for st in both:
-        last_sweep(st)
+        window_sweep(st, st.base, window)
 
     loads[4].wait()
     owners = own_v[...]
@@ -794,12 +787,28 @@
     row24 = lax.broadcasted_iota(I32, (CAP, LN), 0)
     live = row24 < count
 
-    def emit(z):
-        for h in range(2):
-            lanes = pl.ds(pl.multiple_of(z * 256 + h * LN, LN), LN)
-            out[:, lanes] = jnp.where(live, window[2 * z + h, pl.ds(at, CAP), :], 0.0)
-
-    steps(BE, emit)
+    arrive(group_copies)
+    part = group_total[0]
+    for i in range(1, n_grp):
+        part = part + group_total[i]
+    level = part[0:1, 0:1] / part[0:1, 64:65]
+    level = jnp.broadcast_to(level, (CAP, LN))
+
+    out_copies = []
+    for q in range(4):
+        def emit(i, q=q):
+            z = 4 * q + i
+            for h in range(2):
+                lanes = pl.ds(pl.multiple_of(z * 256 + h * LN, LN), LN)
+                rows = pl.ds(at, CAP)
+                v = window[2 * z + h, rows, :] + level * window_w[2 * z + h, rows, :]
+                out_v[:, lanes] = jnp.where(live, v, 0.0)
+
+        steps(4, emit)
+        part = pl.ds(1024 * q, 1024)
+        copy = pltpu.make_async_copy(out_v.at[:, part], out.at[:, part], o_sem.at[q])
+        copy.start()
+        out_copies.append(copy)
 
     for slot in range(N_X):
         finish(face_copies(slot))
@@ -807,6 +816,8 @@
         finish(ghost_copies(slot) + field_copies(slot))
     finish(field_copies(3))
     finish(coupling_copies() + link_copies + share_copies + total_copies + group_copies)
+    for copy in out_copies:
+        copy.wait()
 
 
 def local(potential, right_side, permeability, new_owner, neighbours):
@@ -864,7 +875,10 @@
         vmem((n_sub, 8, LN), F32),
         vmem((n_grp, 8, LN), F32),
         vmem((32, 40, LN), F32),
+        vmem((32, 40, LN), F32),
+        vmem((CAP, 4096), F32),
         dma((5,)),
+        dma((4,)),
         dma((N_X, 2)),
         dma((N_X, 2)),
         dma((4,)),
@@ -886,7 +900,7 @@
         functools.partial(kernel, n_grp, n_sub, nblk),
         out_shape=jax.ShapeDtypeStruct((CAP, 4096), F32),
         in_specs=[pl.BlockSpec(memory_space=pl.ANY)] * 5,
-        out_specs=pl.BlockSpec(memory_space=pltpu.VMEM),
+        out_specs=pl.BlockSpec(memory_space=pl.ANY),
         scratch_shapes=scratch,
         compiler_params=pltpu.CompilerParams(
             collective_id=0, has_side_effects=True, vmem_limit_bytes=60 * 1024 * 1024

time: 35.2 us -> 35.1 us (level)
  no operation moved by 1% of the time
where the time goes in v4:
time: 35.1 us; the launch traced here: 34.9 us
  Pallas kernels  33.2 us (95%)
  local copies, waits for them, and re-layouts  1.77 us (5%)
    pallas_call x1, Pallas kernels, local(): pl.pallas_call(functools.partial(kernel, n_grp, n_sub, nblk), out_shape=j...  33.2 us
    unnamed x1, local copies, waits for them, and re-layouts  1.77 us

profile of v4, /device:TPU:1, one launch (start us, length us, event | category | flops | bytes accessed | tf_op | source)
XLA Modules:
  0.0 34.9 jit_solution(1893273589298130523)
XLA Ops:
  0.0 33.2 %cycle.1 = f32[24,4096]{1,0:T(8,128)} custom-call(f32[16,4096]{1,0:T(8,128)} %pot.1, f32[16,4096]{1,0:T(8,128)} %rs.1, f32[16,4096]{1,0:T(8,128)} %mu.1, s32[16,128]{1,0:T(8,128)} %bitcast.1, s32[6,2048]{1,0:T(8,128)} %neigh.1), custom_call_target="tpu_custom_call" | custom-call | flops 8000000 | bytes 1200000 | tf_op jit(solution)/shard_map/cycle/pallas_call | solution.py:899
  33.2 1.8 %copy.7 = f32[24,4096]{1,0:T(8,128)} copy(f32[24,4096]{1,0:T(8,128)} %cycle.1) | data formatting | bytes 786432

commit v5 on v4

--- a/solution.py
+++ b/solution.py
@@ -660,10 +660,6 @@
     each_plane(sweep_first(rim))
     coefficients(rim)
     inner_sweep(rim, rim.u, rim.base, True)
-    rim_ghosts(1)
-    each_plane(outer_sweep(rim, rim.base, rim.u))
-    inner_sweep(rim, rim.u, rim.base, True)
-
     arrive(total_copies)
     part = total[0]
     for i in range(1, n_sub):
@@ -674,6 +670,10 @@
         for i in range(1, n_grp)
     ]
     start(group_copies)
+
+    rim_ghosts(1)
+    each_plane(outer_sweep(rim, rim.base, rim.u))
+    inner_sweep(rim, rim.u, rim.base, True)
 
     arrive(link_copies)
     iw = lax.broadcasted_iota(I32, (WIN, WIN), 0)

time: 35.1 us -> 35.1 us (level)
  no operation moved by 1% of the time
where the time goes in v5:
time: 35.1 us; the launch traced here: 34.9 us
  Pallas kernels  33.2 us (95%)
  local copies, waits for them, and re-layouts  1.77 us (5%)
    pallas_call x1, Pallas kernels, local(): pl.pallas_call(functools.partial(kernel, n_grp, n_sub, nblk), out_shape=j...  33.2 us
    unnamed x1, local copies, waits for them, and re-layouts  1.77 us

profile of v5, /device:TPU:1, one launch (start us, length us, event | category | flops | bytes accessed | tf_op | source)
XLA Modules:
  0.0 34.9 jit_solution(10472571813620992453)
XLA Ops:
  0.0 33.2 %cycle.1 = f32[24,4096]{1,0:T(8,128)} custom-call(f32[16,4096]{1,0:T(8,128)} %pot.1, f32[16,4096]{1,0:T(8,128)} %rs.1, f32[16,4096]{1,0:T(8,128)} %mu.1, s32[16,128]{1,0:T(8,128)} %bitcast.1, s32[6,2048]{1,0:T(8,128)} %neigh.1), custom_call_target="tpu_custom_call" | custom-call | flops 8000000 | bytes 1200000 | tf_op jit(solution)/shard_map/cycle/pallas_call | solution.py:899
  33.2 1.8 %copy.7 = f32[24,4096]{1,0:T(8,128)} copy(f32[24,4096]{1,0:T(8,128)} %cycle.1) | data formatting | bytes 786432
